TPU v7x, 32 devices: a whole 2x2x4 slice. The times are simulated.
32 devices in a mesh: sp: 8 (over y, x, core), ch: 4 (over z).
Axes of the slice: x: 2, y: 2, z: 4, core: 2. Of those that a mesh axis runs over, the one named last changes fastest.
Arguments:
- volume: bfloat16 [256, 16, 8, 128], P('ch', 'sp'), may hold values from -6 to 6
- filters: bfloat16 [256, 3, 3, 3, 256], P('ch'), may hold values from -0.078125 to 0.078125
- cotangent: bfloat16 [256, 16, 8, 128], P('ch', 'sp'), may hold values from -6 to 6
Outputs:
- response: bfloat16 [256, 16, 8, 128], P('ch', 'sp')
- input_grad: bfloat16 [256, 16, 8, 128], P('ch', 'sp')
- filter_grad: bfloat16 [256, 3, 3, 3, 256], P('ch')
All inputs are finite; a program needn't handle non-finite values.
Results may differ from a plain program's by a relative error of at most 0.0024.
Values may be sent and summed in bfloat16 or wider, within the bound.
A program may use at most 64 MiB of HBM per device.

v0:
```python
import math

import jax
import jax.numpy as jnp
from jax import lax
from jax.sharding import PartitionSpec as P


def extended(value, sides, width):
    for axis, dim in sides:
        size, length = (lax.axis_size(axis), value.shape[dim])
        up = [(i, (i + 1) % size) for i in range(size - 1)]
        down = [(j, i) for i, j in up]
        last = lax.slice_in_dim(value, length - width, length, axis=dim)
        first = lax.slice_in_dim(value, 0, width, axis=dim)
        before = lax.ppermute(last, axis, up)
        after = lax.ppermute(first, axis, down)
        value = jnp.concatenate([before, value, after], axis=dim)
    return value


def place_taps(total, product, flipped):
    height = total.shape[2]
    width = total.shape[3]
    padded = jnp.pad(product, ((0, 0), (0, 0), (0, 0), (0, 0), (1, 1), (1, 1)))
    for row_tap in range(3):
        for col_tap in range(3):
            row_from = 2 - row_tap if flipped else row_tap
            col_from = 2 - col_tap if flipped else col_tap
            total = (
                total
                + padded[
                    row_tap,
                    col_tap,
                    :,
                    :,
                    row_from : row_from + height,
                    col_from : col_from + width,
                ]
            )
    return total


def forward_terms(filters, total, piece):
    count = piece.shape[0]
    outputs = filters.shape[0]
    depth, height, width = (total.shape[1], total.shape[2], total.shape[3])
    for depth_tap in range(3):
        rows = piece[:, depth_tap : depth_tap + depth].reshape(count, -1)
        taps = jnp.transpose(filters[:, depth_tap], (1, 2, 3, 0)).reshape(9, count, outputs)
        product = lax.dot_general(
            taps, rows, (((1,), (0,)), ((), ())), preferred_element_type=jnp.float32
        )
        total = place_taps(total, product.reshape(3, 3, outputs, depth, height, width), False)
    return total


def data_terms(swapped, total, piece):
    count = piece.shape[0]
    channels = swapped.shape[4]
    depth, height, width = (total.shape[1], total.shape[2], total.shape[3])
    for depth_tap in range(3):
        rows = piece[:, 2 - depth_tap : 2 - depth_tap + depth].reshape(count, -1)
        taps = jnp.transpose(swapped[:, depth_tap], (1, 2, 3, 0)).reshape(9, channels, count)
        product = lax.dot_general(
            taps, rows, (((2,), (0,)), ((), ())), preferred_element_type=jnp.float32
        )
        total = place_taps(total, product.reshape(3, 3, channels, depth, height, width), True)
    return total


def filter_terms(shifted, depth, piece):
    count = piece.shape[0]
    outputs = shifted.shape[1]
    blocks = []
    for depth_tap in range(3):
        rows = piece[:, depth_tap : depth_tap + depth].reshape(count, -1)
        block = lax.dot_general(
            rows, shifted, (((1,), (2,)), ((), ())), preferred_element_type=jnp.float32
        )
        blocks.append(jnp.transpose(block, (2, 1, 0)).reshape(outputs, 3, 3, count))
    return jnp.stack(blocks, axis=1)


def local(volume, filters, cotangent):
    depth, height, width = (volume.shape[1], volume.shape[2], volume.shape[3])
    outputs = filters.shape[0]
    local_chan = volume.shape[0]
    planes_all = depth * lax.axis_size("sp")
    rimmed = extended(volume, (("sp", 1),), 1)
    grad_padded = jnp.pad(cotangent, ((0, 0), (0, 0), (1, 1), (1, 1)))
    shifted = jnp.stack(
        [
            grad_padded[
                :, :, 2 - row_tap : 2 - row_tap + height, 2 - col_tap : 2 - col_tap + width
            ].reshape(outputs, -1)
            for row_tap in range(3)
            for col_tap in range(3)
        ]
    )
    start_resp = jnp.zeros((outputs, depth, height, width), jnp.float32)
    response_sum = forward_terms(
        filters, start_resp, lax.all_gather(rimmed, "ch", axis=0, tiled=True)
    )
    kernel_part = filter_terms(shifted, depth, lax.all_gather(rimmed, "ch", axis=0, tiled=True))
    swapped = lax.all_to_all(filters, "ch", split_axis=4, concat_axis=0, tiled=True)
    start_data = jnp.zeros((local_chan, depth, height, width), jnp.float32)
    grad_rimmed = extended(cotangent, (("sp", 1),), 1)
    data_sum = data_terms(
        swapped, start_data, lax.all_gather(grad_rimmed, "ch", axis=0, tiled=True)
    )
    kernel_total = lax.psum(kernel_part, "sp")
    factor = 1.0 / math.sqrt(planes_all * height * width)
    return (
        response_sum.astype(jnp.bfloat16),
        data_sum.astype(jnp.bfloat16),
        (kernel_total * factor).astype(jnp.bfloat16),
    )


def solution(mesh):
    in_specs = (
        P("ch", "sp", None, None),
        P("ch", None, None, None, None),
        P("ch", "sp", None, None),
    )
    out_specs = (
        P("ch", "sp", None, None),
        P("ch", "sp", None, None),
        P("ch", None, None, None, None),
    )
    return jax.shard_map(local, mesh=mesh, in_specs=in_specs, out_specs=out_specs, check_vma=False)
```

profile of v0, /device:TPU:1, one launch (start us, length us, event | category | flops | bytes accessed | tf_op | source)
XLA Modules:
  0.0 215.4 jit_solution(12273264293442405348)
XLA Ops:
  7.2 1.1 fusion.82
  8.3 4.5 %collective-permute-start.2 = (bf16[64,1,8,128]{3,2,1,0:T(8,128)(2,1)S(1)}, bf16[64,1,8,128]{3,2,1,0:T(8,128)(2,1)S(1)}, u32[]{:S(2)}, u32[]{:S(2)}) collective-permute-start(bf16[64,1,8,128]{3,2,1,0:T(8,128)(2,1)S(1)} %get-tuple-element.23), channel_id=1, source_target_pairs={{0,4},{4,8},{8,12},{12,16},{16,20},{20,24},{24,28},{1,5},{5,9},{9,... | collective-permute-start | bytes 393224 | tf_op jit(solution)/shard_map/ppermute | solution.py:16
  12.8 1.9 collective-permute-start.3
  14.8 4.3 %collective-permute-done.3 = bf16[64,1,8,128]{3,2,1,0:T(8,128)(2,1)S(1)} collective-permute-done((bf16[64,1,8,128]{3,2,1,0:T(8,128)(2,1)S(1)}, bf16[64,1,8,128]{3,2,1,0:T(8,128)(2,1)S(1)}, u32[]{:S(2)}, u32[]{:S(2)}) %collective-permute-start.3) | collective-permute-done | bytes 131104 | tf_op jit(solution)/shard_map/ppermute | solution.py:17
  19.1 1.9 pad_maximum_fusion.2
  21.0 1.0 fusion.83
  22.0 1.9 collective-permute-start
  24.0 2.4 %collective-permute-start.1 = (bf16[64,1,8,128]{3,2,1,0:T(8,128)(2,1)S(1)}, bf16[64,1,8,128]{3,2,1,0:T(8,128)(2,1)S(1)}, u32[]{:S(2)}, u32[]{:S(2)}) collective-permute-start(bf16[64,1,8,128]{3,2,1,0:T(8,128)(2,1)S(1)} %get-tuple-element.26), channel_id=1, source_target_pairs={{4,0},{8,4},{12,8},{16,12},{20,16},{24,20},{28,24},{5,1},{9,5},{13... | collective-permute-start | bytes 393224 | tf_op jit(solution)/shard_map/ppermute | solution.py:17
  26.4 4.6 %collective-permute-done.1 = bf16[64,1,8,128]{3,2,1,0:T(8,128)(2,1)S(1)} collective-permute-done((bf16[64,1,8,128]{3,2,1,0:T(8,128)(2,1)S(1)}, bf16[64,1,8,128]{3,2,1,0:T(8,128)(2,1)S(1)}, u32[]{:S(2)}, u32[]{:S(2)}) %collective-permute-start.1) | collective-permute-done | bytes 131104 | tf_op jit(solution)/shard_map/ppermute | solution.py:17
  31.0 0.9 pad_maximum_fusion.1
  32.0 1.9 copy.7
  33.9 2.7 %reshape.131 = bf16[4,2,55296]{2,1,0:T(2,128)(2,1)} reshape(bf16[256,3,3,3,64]{4,3,2,1,0:T(4,128)(2,1)S(1)} %bitcast.355) | data formatting | bytes 1769472
  36.6 4.6 %all-to-all-start = ((bf16[4,2,55296]{2,1,0:T(2,128)(2,1)}), bf16[4,2,55296]{2,1,0:T(2,128)(2,1)}, u32[]{:S(2)}, u32[]{:S(2)}) async-start(bf16[4,2,55296]{2,1,0:T(2,128)(2,1)} %reshape.131), calls=%async_computation | async-start | bytes 1769472 | tf_op jit(solution)/shard_map/all_to_all | solution.py:106
  41.2 0.8 stack_reshape.40
  50.1 1.0 fusion.81
  51.1 32.9 %all-to-all-done = bf16[4,2,55296]{2,1,0:T(2,128)(2,1)} async-done(((bf16[4,2,55296]{2,1,0:T(2,128)(2,1)}), bf16[4,2,55296]{2,1,0:T(2,128)(2,1)}, u32[]{:S(2)}, u32[]{:S(2)}) %all-to-all-start) | async-done | bytes 884768 | tf_op jit(solution)/shard_map/all_to_all | solution.py:106
  84.0 3.0 %reshape.132 = bf16[256,3,3,3,64]{4,3,2,1,0:T(4,128)(2,1)S(1)} reshape(bf16[4,2,55296]{2,1,0:T(2,128)(2,1)} %all-to-all-done) | data formatting | bytes 1769472
  87.0 2.9 %copy.8 = bf16[4,64,3,3,3,64]{1,0,5,4,3,2:T(4,128)(2,1)} copy(bf16[4,64,3,3,3,64]{1,4,3,2,5,0:T(4,128)(2,1)S(1)} %bitcast.354) | data formatting | bytes 1769472 | tf_op jit(solution)/shard_map/all_to_all | solution.py:106
  90.0 3.1 %all_to_all.16 = bf16[256,3,3,3,64]{0,4,3,2,1:T(8,128)(2,1)S(1)} reshape(bf16[4,64,3,3,3,64]{1,0,5,4,3,2:T(4,128)(2,1)} %copy.8) | data formatting | bytes 1769472 | tf_op jit(solution)/shard_map/all_to_all | solution.py:106
  93.0 0.9 fusion.80
  94.0 2.6 %fusion.78 = (bf16[256,2,8,128]{3,2,1,0:T(8,128)(2,1)S(1)}, bf16[256,2,8,128]{3,2,1,0:T(8,128)(2,1)S(1)}, bf16[256,2,8,128]{3,2,1,0:T(8,128)(2,1)S(1)}) fusion(bf16[256,4,8,128]{3,2,1,0:T(8,128)(2,1)} %all-gather.5.cloned.1.call-done), kind=kLoop, calls=%fused_computation.152 | loop fusion | bytes 6291456 | tf_op jit(solution)/shard_map/slice | solution.py:63
  96.5 1.3 reshape.119
  97.8 1.3 reshape.121
  99.1 1.2 reshape.120
  100.3 32.5 %all-gather.3.cloned.1.call-done = bf16[256,4,8,128]{3,2,1,0:T(8,128)(2,1)} async-done(((bf16[64,4,8,128]{3,2,1,0:T(8,128)(2,1)}), bf16[256,4,8,128]{3,2,1,0:T(8,128)(2,1)}) %all-gather.3.cloned.1.call-update) | async-done | bytes 2097168 | tf_op jit(solution)/shard_map/all_gather | solution.py:103
  132.8 2.4 %fusion.79 = (bf16[256,2,8,128]{3,2,1,0:T(8,128)(2,1)S(1)}, bf16[256,2,8,128]{3,2,1,0:T(8,128)(2,1)S(1)}, bf16[256,2,8,128]{3,2,1,0:T(8,128)(2,1)S(1)}) fusion(bf16[256,4,8,128]{3,2,1,0:T(8,128)(2,1)} %all-gather.3.cloned.1.call-done), kind=kLoop, calls=%fused_computation.153 | loop fusion | bytes 6291456 | tf_op jit(solution)/shard_map/slice | solution.py:49
  135.2 1.3 reshape.122
  136.5 1.3 reshape.124
  137.8 1.3 reshape.123
  139.0 2.9 %fusion.89 = f32[256,9,64]{0,2,1:T(8,128)S(1)} fusion(bf16[256,2048,1]{1,0,2:T(8,128)(2,1)} %reshape.124, bf16[9,64,2048]{2,1,0:T(8,128)(2,1)} %constant_dynamic-update-slice_fusion), kind=kOutput, calls=%fused_computation.163 | convolution fusion | flops 603979776 | bytes 3997696 | tf_op jit(solution)/shard_map/dot_general | solution.py:78
  141.9 2.6 %fusion.88 = f32[256,9,64]{0,2,1:T(8,128)S(1)} fusion(bf16[256,2048,1]{1,0,2:T(8,128)(2,1)S(1)} %copy-done.9, bf16[9,64,2048]{2,1,0:T(8,128)(2,1)} %constant_dynamic-update-slice_fusion), kind=kOutput, calls=%fused_computation.162 | convolution fusion | flops 603979776 | bytes 3997696 | tf_op jit(solution)/shard_map/dot_general | solution.py:78
  144.5 2.5 %fusion.87 = f32[256,9,64]{0,2,1:T(8,128)S(1)} fusion(bf16[256,2048,1]{1,0,2:T(8,128)(2,1)S(1)} %copy-done.8, bf16[9,64,2048]{2,1,0:T(8,128)(2,1)} %constant_dynamic-update-slice_fusion), kind=kOutput, calls=%fused_computation.161 | convolution fusion | flops 603979776 | bytes 3997696 | tf_op jit(solution)/shard_map/dot_general | solution.py:78
  147.0 1.3 pad_maximum_fusion
  148.4 2.1 fusion.86
  150.4 1.1 copy.17
  151.7 0.8 fusion.84
  152.5 1.1 copy.15
  153.8 0.8 fusion.85
  154.6 1.1 copy.16
  155.7 0.8 convolution_bitcast_fusion.1
  156.5 1.1 copy.12
  157.6 0.8 convolution_bitcast_fusion
  158.4 1.1 copy.14
  159.4 1.0 convolution_bitcast_fusion.2
  160.5 3.2 %copy.10 = f32[72,8,16,128]{3,2,1,0:T(8,128)} copy(f32[72,8,16,128]{3,1,2,0:T(8,128)S(1)} %convolution_bitcast_fusion.2) | data formatting | bytes 9437184
  163.7 7.3 %fusion.76 = (bf16[64,2,8,128]{3,2,1,0:T(8,128)(2,1)}, bf16[64,2,8,128]{3,2,1,0:T(8,128)(2,1)}) fusion(f32[3,3,64,2,8,128]{5,4,3,2,1,0:T(8,128)S(1)} %bitcast.348, f32[3,3,64,2,8,128]{5,4,3,2,1,0:T(8,128)S(1)} %bitcast.350, f32[3,3,64,2,8,128]{5,4,3,2,1,0:T(8,128)S(1)} %bitcast.349, f32[3,3,64,2,8,128]{5,4,3,2,1,0:T(8,128)S(1)} %bitcast.352, ...), kind=kLoop, calls=%fused_computation.141 | loop fusion | flops 7077888 | bytes 31981568 | tf_op jit(solution)/shard_map/convert_element_type | solution.py:116
  171.0 35.3 %all-reduce.9.cloned.1.call-done = f32[64,3,3,3,256]{4,0,3,2,1:T(8,128)} async-done(((f32[64,3,3,3,256]{4,0,3,2,1:T(8,128)}), f32[64,3,3,3,256]{4,0,3,2,1:T(8,128)}) %all-reduce.9.cloned.1.call-update) | async-done | bytes 1769488 | tf_op jit(solution)/shard_map/psum | solution.py:112
  206.2 2.6 %multiply_convert_fusion = bf16[64,3,3,3,256]{4,0,3,2,1:T(8,128)(2,1)} fusion(f32[64,3,3,3,256]{4,0,3,2,1:T(8,128)} %all-reduce.9.cloned.1.call-done), kind=kLoop, calls=%fused_computation.60 | loop fusion | flops 884736 | bytes 2654208 | tf_op jit(solution)/shard_map/convert_element_type | solution.py:117
  (51 shorter events, 8.7 us)
Async XLA Ops:
  7.2 23.9 %copy-start.11 = (bf16[64,2,8,128]{3,2,1,0:T(8,128)(2,1)S(1)}, bf16[64,2,8,128]{3,2,1,0:T(8,128)(2,1)}, u32[]{:S(2)}) copy-start(bf16[64,2,8,128]{3,2,1,0:T(8,128)(2,1)} %param.3) | copy-start | bytes 786436
  7.2 24.8 %copy-start.3 = (bf16[64,3,3,3,256]{4,0,3,2,1:T(8,128)(2,1)S(1)}, bf16[64,3,3,3,256]{4,0,3,2,1:T(8,128)(2,1)}, u32[]{:S(2)}) copy-start(bf16[64,3,3,3,256]{4,0,3,2,1:T(8,128)(2,1)} %param.4) | copy-start | bytes 2654212
  7.2 86.8 %all-gather.5.cloned.1.call-start = ((), (), s32[]{:S(2)}) async-start(), calls=%async_computation.2 | async-start | bytes 2621440 | tf_op jit(solution)/shard_map/all_gather | solution.py:110
  8.3 6.4 %collective-permute-start.2 = (bf16[64,1,8,128]{3,2,1,0:T(8,128)(2,1)S(1)}, bf16[64,1,8,128]{3,2,1,0:T(8,128)(2,1)S(1)}, u32[]{:S(2)}, u32[]{:S(2)}) collective-permute-start(bf16[64,1,8,128]{3,2,1,0:T(8,128)(2,1)S(1)} %get-tuple-element.23), channel_id=1, source_target_pairs={{0,4},{4,8},{8,12},{12,16},{16,20},{20,24},{24,28},{1,5},{5,9},{9,... | collective-permute-start | bytes 393224 | tf_op jit(solution)/shard_map/ppermute | solution.py:16
  12.8 6.3 %collective-permute-start.3 = (bf16[64,1,8,128]{3,2,1,0:T(8,128)(2,1)S(1)}, bf16[64,1,8,128]{3,2,1,0:T(8,128)(2,1)S(1)}, u32[]{:S(2)}, u32[]{:S(2)}) collective-permute-start(bf16[64,1,8,128]{3,2,1,0:T(8,128)(2,1)S(1)} %get-tuple-element.24), channel_id=1, source_target_pairs={{4,0},{8,4},{12,8},{16,12},{20,16},{24,20},{28,24},{5,1},{9,5},{13... | collective-permute-start | bytes 393224 | tf_op jit(solution)/shard_map/ppermute | solution.py:17
  21.0 111.8 %all-gather.3.cloned.1.call-start = ((), (), s32[]{:S(2)}) async-start(), calls=%async_computation.1 | async-start | bytes 2621440 | tf_op jit(solution)/shard_map/all_gather | solution.py:103
  22.0 4.3 %collective-permute-start = (bf16[64,1,8,128]{3,2,1,0:T(8,128)(2,1)S(1)}, bf16[64,1,8,128]{3,2,1,0:T(8,128)(2,1)S(1)}, u32[]{:S(2)}, u32[]{:S(2)}) collective-permute-start(bf16[64,1,8,128]{3,2,1,0:T(8,128)(2,1)S(1)} %get-tuple-element.25), channel_id=1, source_target_pairs={{0,4},{4,8},{8,12},{12,16},{16,20},{20,24},{24,28},{1,5},{5,9},{9,... | collective-permute-start | bytes 393224 | tf_op jit(solution)/shard_map/ppermute | solution.py:16
  24.0 7.0 %collective-permute-start.1 = (bf16[64,1,8,128]{3,2,1,0:T(8,128)(2,1)S(1)}, bf16[64,1,8,128]{3,2,1,0:T(8,128)(2,1)S(1)}, u32[]{:S(2)}, u32[]{:S(2)}) collective-permute-start(bf16[64,1,8,128]{3,2,1,0:T(8,128)(2,1)S(1)} %get-tuple-element.26), channel_id=1, source_target_pairs={{4,0},{8,4},{12,8},{16,12},{20,16},{24,20},{28,24},{5,1},{9,5},{13... | collective-permute-start | bytes 393224 | tf_op jit(solution)/shard_map/ppermute | solution.py:17
  33.9 7.3 %copy-start = (bf16[64,2,8,128]{3,2,1,0:T(8,128)(2,1)S(1)}, bf16[64,2,8,128]{3,2,1,0:T(8,128)(2,1)}, u32[]{:S(2)}) copy-start(bf16[64,2,8,128]{3,2,1,0:T(8,128)(2,1)} %param.5) | copy-start | bytes 786436
  36.6 47.4 %all-to-all-start = ((bf16[4,2,55296]{2,1,0:T(2,128)(2,1)}), bf16[4,2,55296]{2,1,0:T(2,128)(2,1)}, u32[]{:S(2)}, u32[]{:S(2)}) async-start(bf16[4,2,55296]{2,1,0:T(2,128)(2,1)} %reshape.131), calls=%async_computation | async-start | bytes 1769472 | tf_op jit(solution)/shard_map/all_to_all | solution.py:106
  41.2 165.1 %all-reduce.9.cloned.1.call-start = ((), (), s32[]{:S(2)}) async-start(), calls=%async_computation.3 | async-start | bytes 3538944 | tf_op jit(solution)/shard_map/psum | solution.py:112
  42.9 3.5 %copy-start.10 = (bf16[1,64,2048]{2,1,0:T(8,128)(2,1)S(1)}, bf16[1,64,2048]{2,1,0:T(8,128)(2,1)}, u32[]{:S(2)}) copy-start(bf16[1,64,2048]{2,1,0:T(8,128)(2,1)} %stack_reshape.40) | copy-start | bytes 786436
  139.0 2.9 %copy-start.9 = (bf16[256,2048,1]{1,0,2:T(8,128)(2,1)S(1)}, bf16[256,2048,1]{1,0,2:T(8,128)(2,1)}, u32[]{:S(2)}) copy-start(bf16[256,2048,1]{1,0,2:T(8,128)(2,1)} %reshape.123) | copy-start | bytes 3145732
  141.9 2.6 %copy-start.8 = (bf16[256,2048,1]{1,0,2:T(8,128)(2,1)S(1)}, bf16[256,2048,1]{1,0,2:T(8,128)(2,1)}, u32[]{:S(2)}) copy-start(bf16[256,2048,1]{1,0,2:T(8,128)(2,1)} %reshape.122) | copy-start | bytes 3145732
  150.4 1.2 copy-start.2
  150.4 1.3 copy-start.7
  152.5 1.3 copy-start.1
  154.6 1.1 copy-start.6
  156.5 1.1 copy-start.5
  158.4 1.1 copy-start.4
Sparse Core Ops, SparseCore 0:
  21.1 65.3 all-gather.4
  88.1 44.6 all-gather.2
  148.5 57.7 all-reduce.8
where the time goes:
time: 217 us; the launch traced here: 215 us
  waiting for transfers between devices  110 us (51%)
  local copies, waits for them, and re-layouts  48 us (22%)
  starting transfers between devices  15.4 us (7%)
  matrix products  14.1 us (6%)
  between operations  14.1 us (6%)
  other arithmetic  14 us (6%)
    psum x1, waiting for transfers between devices, local(): kernel_total = lax.psum(kernel_part, 'sp')  35.3 us
    all_to_all x1, waiting for transfers between devices, local(): lax.all_to_all(filters, 'ch', split_axis=4, concat_axis=0, tiled=True)  32.9 us
    all_gather x1, waiting for transfers between devices, local(): lax.all_gather(rimmed, 'ch', axis=0, tiled=True)  32.5 us
    unnamed x41, local copies, waits for them, and re-layouts  22.5 us
    ppermute x2, waiting for transfers between devices, extended(): after = lax.ppermute(first, axis, down)  8.97 us
    dot_general x3, matrix products, filter_terms(): lax.dot_general(rows, shifted, (((1,), (2,)), ((), ())), preferred_elemen...  7.91 us
    convert_element_type x1, other arithmetic, local(): data_sum.astype(jnp.bfloat16)  7.32 us
    ppermute x2, starting transfers between devices, extended(): before = lax.ppermute(last, axis, up)  6.43 us
  transfers between devices with their start and end apart: 8, of which 5 were waited for; matrix products, arithmetic and copies ran while one was open for 24% of the time, Pallas kernels for 0%

commit v1 on v0

v1 whole, which is shorter than its diff:
```python
import functools
import math

import jax
import jax.numpy as jnp
from jax import lax
from jax.experimental import pallas as pl
from jax.experimental.pallas import tpu as pltpu
from jax.sharding import PartitionSpec as P

BF = jnp.bfloat16
F32 = jnp.float32


def shifts(x, width):
    wide = x.astype(F32)
    lane = lax.broadcasted_iota(jnp.int32, x.shape, 1) % width
    before = jnp.where(lane == 0, 0.0, pltpu.roll(wide, 1, 1)).astype(BF)
    after = jnp.where(lane == width - 1, 0.0, pltpu.roll(wide, x.shape[1] - 1, 1)).astype(BF)
    return before, after


def kernel(
    n, S, D, H, W, gpc, factor,
    vol, cot, wfwd, sendw,
    resp, igrad, fout,
    vall, call, edge, crim, racc, iacc, rbuf, ibuf, wsb, wst, fpart, rs1, rs2, fog,
    zs, zr, ws1, wr1, ws2, wr2, cs, cr, rims, rimr, f1s, f1r, f2s, f2r, a1s, a1r, a2s, a2r,
):
    i, s = lax.axis_index("ch"), lax.axis_index("sp")
    cb, cells = vol.shape
    fb = cot.shape[0]
    F = fb * n
    HW = H * W
    G = 3 * gpc
    half = S // 2
    m, e = s // 2, s % 2
    sib = m * 2 + 1 - e

    bar = pltpu.get_barrier_semaphore()
    for d in range(1, n):
        pl.semaphore_signal(bar, inc=1, device_id={"ch": (i + d) % n}, device_id_type=pl.DeviceIdType.MESH)
    for d in range(1, S):
        pl.semaphore_signal(bar, inc=1, device_id={"sp": (s + d) % S}, device_id_type=pl.DeviceIdType.MESH)
    pl.semaphore_wait(bar, n + S - 2)

    def remote(src, dst, ssem, rsem, dev):
        return pltpu.make_async_remote_copy(
            src_ref=src, dst_ref=dst, send_sem=ssem, recv_sem=rsem,
            device_id=dev, device_id_type=pl.DeviceIdType.MESH,
        )

    def rows(j, size):
        return pl.ds(pl.multiple_of(j * size, size), size)

    def zcopy(which, direction, t):
        buf, own = ((vall, vol), (call, cot))[which]
        size = own.shape[0]
        block = i - t if direction == 0 else i + t
        spot = buf.at[1, rows(block, size), :]
        src = own if t == 0 else spot
        to = i + 1 if direction == 0 else i - 1
        return remote(src, spot, zs.at[which, direction, t], zr.at[which, direction, t], {"ch": to})

    def zsends(direction, t):
        return (i < n - 1) & (i - t >= 0) if direction == 0 else (i > 0) & (i + t <= n - 1)

    def zrecvs(direction, t):
        return i - 1 - t >= 0 if direction == 0 else i + 1 + t <= n - 1

    def zstart(which, t):
        for direction in range(2):
            @pl.when(zsends(direction, t))
            def _():
                zcopy(which, direction, t).start()

    def zwait(which, t):
        buf, own = ((vall, vol), (call, cot))[which]
        size = own.shape[0]
        for direction in range(2):
            @pl.when(zrecvs(direction, t))
            def _():
                block = i - 1 - t if direction == 0 else i + 1 + t
                spot = buf.at[1, rows(block, size), :]
                remote(spot, spot, zs.at[which, direction, t], zr.at[which, direction, t], {"ch": (i + 1) % n}).wait_recv()

    def zshift(which, t):
        buf, own = ((vall, vol), (call, cot))[which]
        size = own.shape[0]
        for direction in range(2):
            @pl.when(zrecvs(direction, t))
            def _():
                block = i - 1 - t if direction == 0 else i + 1 + t
                place = rows(block, size)
                before, after = shifts(buf[1, place, :], W)
                buf[0, place, :] = before if which == 0 else after
                buf[2, place, :] = after if which == 0 else before

    def zfinish(which, t):
        for direction in range(2):
            @pl.when(zsends(direction, t))
            def _():
                zcopy(which, direction, t).wait_send()

    def crim_copy(up):
        plane = cot.at[:, (D - 1) * HW : D * HW] if up else cot.at[:, 0:HW]
        k = 0 if up else 1
        return remote(plane, crim.at[k], cs.at[k], cr.at[k], {"sp": s + 1 if up else s - 1})

    def rim_copy(which, up):
        acc, buf = ((racc, rbuf), (iacc, ibuf))[which]
        k = 0 if up else 1
        src = acc.at[D + 1 if up else 0, :, W : W + HW]
        return remote(src, buf.at[k], rims.at[which, k], rimr.at[which, k], {"sp": s + 1 if up else s - 1})

    def both_ways(act):
        @pl.when(s < S - 1)
        def _():
            act(True)

        @pl.when(s > 0)
        def _():
            act(False)

    carried = -(-G // S)

    def w1_copy(r, d):
        g = s + r * S
        return remote(
            sendw.at[(i + d) % n, g], wsb.at[g, rows(i, fb), :], ws1.at[r, d - 1], wr1.at[r, d - 1], {"ch": (i + d) % n}
        )

    def w2_copy(r, d, g):
        return remote(wsb.at[g], wsb.at[g], ws2.at[r, d - 1], wr2.at[r, d - 1], {"sp": (s + d) % S})

    def w_mine(act):
        for r in range(carried):
            @pl.when(s + r * S < G)
            def _():
                act(r, s + r * S)

    zstart(0, 0)
    both_ways(lambda up: crim_copy(up).start())

    def w1_go(r, g):
        for d in range(1, n):
            w1_copy(r, d).start()
        wsb[g, rows(i, fb), :] = sendw[i, g]

    w_mine(w1_go)

    x = vol[...]
    before, after = shifts(x, W)
    vall[0, rows(i, cb), :] = before
    vall[1, rows(i, cb), :] = x
    vall[2, rows(i, cb), :] = after
    x = cot[...]
    before, after = shifts(x, W)
    call[0, rows(i, fb), :] = after
    call[1, rows(i, fb), :] = x
    call[2, rows(i, fb), :] = before
    edge[...] = jnp.zeros_like(edge)
    for c, part in enumerate((after, x, before)):
        for z in range(D):
            edge[c, z + 1, :, W : W + HW] = part[:, z * HW : (z + 1) * HW]
    racc[...] = jnp.zeros_like(racc)
    iacc[...] = jnp.zeros_like(iacc)

    def w2_go(r, g):
        for d in range(1, n):
            w1_copy(r, d).wait()
        for d in range(1, S):
            w2_copy(r, d, g).start()

    def crim_use(up):
        pass

    def early():
        w_mine(w2_go)

        @pl.when(s > 0)
        def _():
            remote(crim.at[0], crim.at[0], cs.at[0], cr.at[0], {"sp": (s + 1) % S}).wait_recv()
            x = crim[0]
            before, after = shifts(x, W)
            for c, part in enumerate((after, x, before)):
                edge[c, 0, :, W : W + HW] = part

        @pl.when(s < S - 1)
        def _():
            remote(crim.at[1], crim.at[1], cs.at[1], cr.at[1], {"sp": (s + 1) % S}).wait_recv()
            x = crim[1]
            before, after = shifts(x, W)
            for c, part in enumerate((after, x, before)):
                edge[c, D + 1, :, W : W + HW] = part

    for t in range(n - 1):
        zwait(0, t)
        if t + 1 < n - 1:
            zstart(0, t + 1)
        if t + 1 >= n - 2:
            if t + 1 == max(n - 2, 1):
                zstart(1, 0)
        zshift(0, t)
        if t == 0:
            early()

    R = fpart.shape[2]

    def fgrad():
        def body(step, _):
            a, c = step // 3, step % 3
            total = jnp.zeros((3 * fb, n * cb), F32)
            for z in range(D):
                plane = z + 2 - a
                left = jnp.concatenate(
                    [edge[c, plane, :, (2 - b) * W : (2 - b) * W + HW] for b in range(3)], axis=0
                )
                total += lax.dot_general(
                    left, vall[1, :, z * HW : (z + 1) * HW], (((1,), (1,)), ((), ())), preferred_element_type=F32
                )
            fflat[pl.ds(pl.multiple_of(step * 3 * fb, 8), 3 * fb), :] = total
            return 0

        lax.fori_loop(0, 9, body, 0)

    fflat = fpart.reshape(2 * half * R, n * cb)
    if 27 * fb < 2 * half * R:
        fflat[27 * fb :, :] = jnp.zeros((2 * half * R - 27 * fb, n * cb), F32)
    fgrad()

    def f1_copy():
        return remote(fpart.at[1 - e], rs1, f1s, f1r, {"sp": sib})

    f1_copy().start()

    tile = 2 * W if H % 2 == 0 else W
    per_plane = HW // tile

    def conv(weights, source, acc, size, forward):
        def body(step, _):
            z, q = step // per_plane, step % per_plane
            lanes = pl.ds(pl.multiple_of(step * tile, W), tile)
            right = source[:, :, lanes].reshape(3 * source.shape[1], tile)
            product = jnp.dot(weights[...], right, preferred_element_type=F32)
            for a in range(3):
                plane = z + 2 - a if forward else z + a
                for b in range(3):
                    off = 2 - b if forward else b
                    spot = pl.ds(pl.multiple_of(q * tile + off * W, W), tile)
                    k = 3 * a + b
                    acc[plane, :, spot] += product[k * size : (k + 1) * size]
            return 0

        lax.fori_loop(0, D * per_plane, body, 0)

    def response():
        conv(wfwd, vall, racc, fb, True)
        both_ways(lambda up: rim_copy(0, up).start())

    def f2_copy(d):
        to = ((m + d) % half) * 2 + e
        return remote(fpart.at[e, (m + d) % half], rs2.at[d - 1], f2s.at[d - 1], f2r.at[d - 1], {"sp": to})

    def reduce_pair():
        f1_copy().wait()
        fpart[e] = fpart[e] + rs1[...]
        for d in range(1, half):
            f2_copy(d).start()

    def a1_copy(d):
        spot = fog.at[e, m]
        return remote(spot, spot, a1s.at[d - 1], a1r.at[d - 1], {"sp": ((m + d) % half) * 2 + e})

    def a2_copy(d):
        spot = fog.at[e, (m - d + half) % half]
        return remote(spot, spot, a2s.at[d], a2r.at[d], {"sp": sib})

    def reduce_chips():
        total = fpart[e, m]
        for d in range(1, half):
            f2_copy(d).wait()
            total = total + rs2[d - 1]
        fog[e, m] = (total * factor).astype(BF)
        for d in range(1, half):
            a1_copy(d).start()
        a2_copy(0).start()

    def kernel_swapped():
        for r in range(carried):
            for d in range(1, S):
                g = (s - d + S) % S + r * S

                @pl.when(g < G)
                def _():
                    w2_copy(r, d, g).wait_recv()

        for c in range(3):
            for g in range(gpc):
                wst[g * W : (g + 1) * W, c * F : (c + 1) * F] = wsb[c * gpc + g].T

    def finish(which, out, acc, buf):
        @pl.when(s > 0)
        def _():
            remote(buf.at[0], buf.at[0], rims.at[which, 0], rimr.at[which, 0], {"sp": (s + 1) % S}).wait_recv()
            acc[1, :, W : W + HW] += buf[0]

        @pl.when(s < S - 1)
        def _():
            remote(buf.at[1], buf.at[1], rims.at[which, 1], rimr.at[which, 1], {"sp": (s + 1) % S}).wait_recv()
            acc[D, :, W : W + HW] += buf[1]

        for z in range(D):
            out[:, z * HW : (z + 1) * HW] = acc[z + 1, :, W : W + HW].astype(BF)

    def gather_forward():
        for d in range(1, half):
            a1_copy(d).wait_recv()
            a2_copy(d).start()

    work = [[response, kernel_swapped], [reduce_pair], [reduce_chips]]
    at = {}
    for k, items in enumerate(work):
        at.setdefault(min(k, max(n - 2, 0)), []).extend(items)
    for t in range(n - 1):
        zwait(1, t)
        if t + 1 < n - 1:
            zstart(1, t + 1)
        zshift(1, t)
        if t < n - 2:
            for item in at.get(t, []):
                item()
    for item in at.get(n - 2, []):
        if item is not reduce_chips:
            item()

    conv(wst, call, iacc, cb, False)
    both_ways(lambda up: rim_copy(1, up).start())
    reduce_chips()
    finish(0, resp, racc, rbuf)
    gather_forward()
    finish(1, igrad, iacc, ibuf)
    for d in range(half):
        spot = fog.at[1 - e, (m - d + half) % half]
        remote(spot, spot, a2s.at[d], a2r.at[d], {"sp": sib}).wait_recv()
    fout[...] = fog[...]

    for which in range(2):
        for t in range(n - 1):
            zfinish(which, t)
        both_ways(lambda up: rim_copy(which, up).wait_send())
    both_ways(lambda up: crim_copy(up).wait_send())

    def w2_end(r, g):
        for d in range(1, S):
            w2_copy(r, d, g).wait_send()

    w_mine(w2_end)
    for d in range(1, half):
        a1_copy(d).wait_send()
    for d in range(half):
        a2_copy(d).wait_send()


def local(n, S, volume, filters, cotangent):
    cb, D, H, W = volume.shape
    fb = cotangent.shape[0]
    C, F = cb * n, fb * n
    cells = D * H * W
    gpc = -(-9 * cb // W)
    G = 3 * gpc
    half = S // 2
    R = -(-27 * fb // (S * 16)) * 16
    factor = 1.0 / math.sqrt(cells * S)
    taps = filters.reshape(fb, 9, 3, C)
    wfwd = jnp.transpose(taps, (1, 0, 2, 3)).reshape(9 * fb, 3 * C)
    sendw = jnp.transpose(taps.reshape(fb, 9, 3, n, cb), (3, 2, 0, 1, 4)).reshape(n, 3, fb, 9 * cb)
    sendw = jnp.pad(sendw, ((0, 0), (0, 0), (0, 0), (0, gpc * W - 9 * cb)))
    sendw = jnp.transpose(sendw.reshape(n, 3, fb, gpc, W), (0, 1, 3, 2, 4)).reshape(n, G, fb, W)
    dma = pltpu.SemaphoreType.DMA
    spec = pl.BlockSpec(memory_space=pltpu.VMEM)
    carried = -(-G // S)
    pads = (H + 2) * W
    resp, igrad, fgrad = pl.pallas_call(
        functools.partial(kernel, n, S, D, H, W, gpc, factor),
        out_shape=(
            jax.ShapeDtypeStruct((fb, cells), BF),
            jax.ShapeDtypeStruct((cb, cells), BF),
            jax.ShapeDtypeStruct((2, half, R, C), BF),
        ),
        in_specs=[spec] * 4,
        out_specs=(spec,) * 3,
        scratch_shapes=[
            pltpu.VMEM((3, C, cells), BF),
            pltpu.VMEM((3, F, cells), BF),
            pltpu.VMEM((3, D + 2, fb, pads), BF),
            pltpu.VMEM((2, fb, H * W), BF),
            pltpu.VMEM((D + 2, fb, pads), F32),
            pltpu.VMEM((D + 2, cb, pads), F32),
            pltpu.VMEM((2, fb, H * W), F32),
            pltpu.VMEM((2, cb, H * W), F32),
            pltpu.VMEM((G, F, W), BF),
            pltpu.VMEM((gpc * W, 3 * F), BF),
            pltpu.VMEM((2, half, R, C), F32),
            pltpu.VMEM((half, R, C), F32),
            pltpu.VMEM((half - 1, R, C), F32),
            pltpu.VMEM((2, half, R, C), BF),
            dma((2, 2, n - 1)),
            dma((2, 2, n - 1)),
            dma((carried, n - 1)),
            dma((carried, n - 1)),
            dma((carried, S - 1)),
            dma((carried, S - 1)),
            dma((2,)),
            dma((2,)),
            dma((2, 2)),
            dma((2, 2)),
            dma,
            dma,
            dma((half - 1,)),
            dma((half - 1,)),
            dma((half - 1,)),
            dma((half - 1,)),
            dma((half,)),
            dma((half,)),
        ],
        compiler_params=pltpu.CompilerParams(
            collective_id=0, has_side_effects=True, vmem_limit_bytes=50 * 2**20
        ),
    )(volume.reshape(cb, cells), cotangent.reshape(fb, cells), wfwd, sendw)
    fgrad = fgrad.reshape(S * R, C)[: 27 * fb].reshape(3, 3, 3, fb, C)
    return (
        resp.reshape(fb, D, H, W),
        igrad.reshape(cb, D, H, W),
        jnp.transpose(fgrad, (3, 0, 2, 1, 4)),
    )


def solution(mesh):
    n, S = mesh.shape["ch"], mesh.shape["sp"]
    wide = P("ch", "sp", None, None)
    kern = P("ch", None, None, None, None)
    return jax.shard_map(
        functools.partial(local, n, S),
        mesh=mesh,
        in_specs=(wide, kern, wide),
        out_specs=(wide, wide, kern),
        check_vma=False,
    )
```

time: 217 us -> 80.3 us (0.37)
  waiting for transfers between devices: 110 us -> 0 us
  Pallas kernels: 0 us -> 65 us
  local copies, waits for them, and re-layouts: 48 us -> 14.4 us
  starting transfers between devices: 15.4 us -> 0 us
  matrix products: 14.1 us -> 0 us
  other arithmetic: 14 us -> 0 us
  between operations: 14.1 us -> 0.72 us
    pallas_call x0 -> x1, Pallas kernels: none -> 65 us  [local(): pl.pallas_call(functools.partial(kernel, n, S, D, H, W, gpc, factor), out...]
    psum x1 -> x0, waiting for transfers between devices: 35.3 us -> none  [local(): kernel_total = lax.psum(kernel_part, 'sp')]
    all_to_all x1 -> x0, waiting for transfers between devices: 32.9 us -> none  [local(): lax.all_to_all(filters, 'ch', split_axis=4, concat_axis=0, tiled=True)]
    all_gather x2 -> x0, waiting for transfers between devices: 32.5 us -> none  [the longest x1 32.5 us: local(): lax.all_gather(rimmed, 'ch', axis=0, tiled=True)]
    unnamed x41 -> x8, local copies, waits for them, and re-layouts: 22.5 us -> 2.82 us
    dot_general x6 -> x0, matrix products: 11.5 us -> none  [the longest x3 7.91 us: filter_terms(): lax.dot_general(rows, shifted, (((1,), (2,)), ((), ())), preferred_elemen...]
    ppermute x4 -> x0, starting transfers between devices: 10.8 us -> none  [the longest x2 6.43 us: extended(): before = lax.ppermute(last, axis, up)]
    convert_element_type x2 -> x0, other arithmetic: 9.92 us -> none  [the longest x1 7.32 us: local(): data_sum.astype(jnp.bfloat16)]
  transfers between devices with their start and end apart: 8 -> 0, of which waited for: 5 -> 0; matrix products, arithmetic and copies ran while one was open for 24% -> 0% of each run, Pallas kernels for 0% -> 0%
where the time goes in v1:
time: 80.3 us; the launch traced here: 80.1 us
  Pallas kernels  65 us (81%)
  local copies, waits for them, and re-layouts  14.4 us (18%)
    pallas_call x1, Pallas kernels, local(): pl.pallas_call(functools.partial(kernel, n, S, D, H, W, gpc, factor), out...  65 us
    another operation x2, local copies, waits for them, and re-layouts, local(): taps.reshape(fb, 9, 3, n, cb)  5.37 us
    concatenate x2, local copies, waits for them, and re-layouts  3.16 us
    unnamed x8, local copies, waits for them, and re-layouts  2.82 us

profile of v1, /device:TPU:1, one launch (start us, length us, event | category | flops | bytes accessed | tf_op | source)
XLA Modules:
  0.0 80.1 jit_solution(11246303277315482134)
XLA Ops:
  0.6 3.0 %reshape_reshape.3 = bf16[64,9,3,4,64]{4,3,0,2,1:T(4,128)(2,1)S(1)} reshape(bf16[64,3,3,3,256]{4,0,3,2,1:T(8,128)(2,1)} %param.4) | data formatting | bytes 1769472 | tf_op jit(solution)/shard_map/reshape;reshape | solution.py:377
  3.6 2.4 %copy.9 = bf16[64,9,3,4,64]{0,4,1,2,3:T(8,128)(2,1)S(1)} copy(bf16[64,9,3,4,64]{4,3,0,2,1:T(4,128)(2,1)S(1)} %reshape_reshape.3) | data formatting | bytes 1769472 | tf_op jit(solution)/shard_map/reshape;reshape | solution.py:377
  6.0 1.2 %pad_slice_fusion = (bf16[4,3,64,128]{2,3,1,0:T(8,128)(2,1)S(1)}, bf16[4,3,64,128]{2,3,1,0:T(8,128)(2,1)S(1)}, bf16[4,3,64,128]{2,3,1,0:T(8,128)(2,1)S(1)}, bf16...) fusion(bf16[4,3,64,576]{2,3,1,0:T(8,128)(2,1)S(1)} %bitcast.36), kind=kLoop, calls=%fused_computation | loop fusion | bytes 4325376 | tf_op jit(solution)/shard_map/slice.5
  7.2 2.4 %concatenate.3 = bf16[4,3,320,128]{2,3,1,0:T(8,128)(2,1)S(1)} concatenate(bf16[4,3,64,128]{2,3,1,0:T(8,128)(2,1)} %get-tuple-element.16, bf16[4,3,64,128]{2,3,1,0:T(8,128)(2,1)} %get-tuple-element.15, bf16[4,3,64,128]{2,3,1,0:T(8,128)(2,1)S(1)} %get-tuple-element.14, bf16[4,3,64,128]{2,3,1,0:T(8,128)(2,1)S(1)} %get-tuple-element.13, bf16[4,3,64,128]{2,3,1,0:T(8,128)(2,1)S(1)} %get-tuple-element.12), dimensions={2} | concatenate | bytes 1966080 | tf_op jit(solution)/shard_map/concatenate
  9.6 0.0 copy-start.1
  9.6 0.0 copy-start
  9.6 0.8 copy.10
  10.4 0.2 copy-done.1
  10.5 1.1 %copy_bitcast_fusion = (bf16[64,2048]{1,0:T(8,128)(2,1)S(1)}, bf16[64,2048]{1,0:T(8,128)(2,1)S(1)}) fusion(bf16[8,8,16,128]{3,2,1,0:T(8,128)(2,1)S(1)} %bitcast.42, bf16[8,8,16,128]{3,2,1,0:T(8,128)(2,1)} %bitcast.43), kind=kLoop, calls=%fused_computation.1 | loop fusion | bytes 1048576 | tf_op jit(solution)/shard_map/reshape | solution.py:430
  11.6 0.0 copy-done
  11.6 0.8 copy.8
  12.4 0.2 copy.14
  12.6 65.0 %shard_map.58 = (bf16[64,2048]{1,0:T(8,128)(2,1)S(1)}, bf16[64,2048]{1,0:T(8,128)(2,1)S(1)}, bf16[2,4,224,256]{3,2,1,0:T(8,128)(2,1)S(1)}) custom-call(bf16[64,2048]{1,0:T(8,128)(2,1)S(1)} %get-tuple-element.18.vol, bf16[64,2048]{1,0:T(8,128)(2,1)S(1)} %get-tuple-element.17.cot, bf16[576,768]{1,0:T(8,128)(2,1)S(1)} %bitcast.32, ...), custom_call_target="tpu_custom_call" | custom-call | tf_op jit(solution)/shard_map/pallas_call | solution.py:384
  77.6 0.1 slice.32
  77.6 1.0 %copy.11 = bf16[64,3,3,3,256]{4,0,3,2,1:T(8,128)(2,1)} copy(bf16[64,3,3,3,256]{4,0,2,3,1:T(8,128)(2,1)S(1)} %bitcast.38) | data formatting | bytes 1769472
  78.6 0.7 copy.15
  79.3 0.7 copy.16
Async XLA Ops:
  9.6 1.0 %copy-start.1 = (bf16[64,2,8,128]{3,2,1,0:T(8,128)(2,1)S(1)}, bf16[64,2,8,128]{3,2,1,0:T(8,128)(2,1)}, u32[]{:S(2)}) copy-start(bf16[64,2,8,128]{3,2,1,0:T(8,128)(2,1)} %param.5) | copy-start | bytes 786436
  9.6 2.0 %copy-start = (bf16[64,3,3,3,256]{4,0,3,2,1:T(8,128)(2,1)S(1)}, bf16[64,3,3,3,256]{4,0,3,2,1:T(8,128)(2,1)}, u32[]{:S(2)}) copy-start(bf16[64,3,3,3,256]{4,0,3,2,1:T(8,128)(2,1)} %param.4) | copy-start | bytes 2654212

commit v2 on v1

--- a/solution.py
+++ b/solution.py
@@ -22,9 +22,9 @@
 
 def kernel(
     n, S, D, H, W, gpc, factor,
-    vol, cot, wfwd, sendw,
+    vol, cot, filt,
     resp, igrad, fout,
-    vall, call, edge, crim, racc, iacc, rbuf, ibuf, wsb, wst, fpart, rs1, rs2, fog,
+    vall, call, edge, crim, racc, iacc, rbuf, ibuf, wfwd, swb, wsb, wst, fpart, rs1, rs2, fog,
     zs, zr, ws1, wr1, ws2, wr2, cs, cr, rims, rimr, f1s, f1r, f2s, f2r, a1s, a1r, a2s, a2r,
 ):
     i, s = lax.axis_index("ch"), lax.axis_index("sp")
@@ -127,7 +127,7 @@
     def w1_copy(r, d):
         g = s + r * S
         return remote(
-            sendw.at[(i + d) % n, g], wsb.at[g, rows(i, fb), :], ws1.at[r, d - 1], wr1.at[r, d - 1], {"ch": (i + d) % n}
+            swb.at[r, (i + d) % n], wsb.at[g, rows(i, fb), :], ws1.at[r, d - 1], wr1.at[r, d - 1], {"ch": (i + d) % n}
         )
 
     def w2_copy(r, d, g):
@@ -142,10 +142,16 @@
     zstart(0, 0)
     both_ways(lambda up: crim_copy(up).start())
 
+    tpg = W // cb
+
     def w1_go(r, g):
+        c, q = g // gpc, g % gpc
+        taps = [filt[jnp.minimum(q * tpg + u, 8) * 3 + c] for u in range(tpg)]
+        for j in range(n):
+            swb[r, j] = jnp.concatenate([tap[:, j * cb : (j + 1) * cb] for tap in taps], axis=1)
         for d in range(1, n):
             w1_copy(r, d).start()
-        wsb[g, rows(i, fb), :] = sendw[i, g]
+        wsb[g, rows(i, fb), :] = swb[r, i]
 
     w_mine(w1_go)
 
@@ -163,6 +169,9 @@
     for c, part in enumerate((after, x, before)):
         for z in range(D):
             edge[c, z + 1, :, W : W + HW] = part[:, z * HW : (z + 1) * HW]
+    for k in range(9):
+        for c in range(3):
+            wfwd[k * fb : (k + 1) * fb, c * cb * n : (c + 1) * cb * n] = filt[3 * k + c]
     racc[...] = jnp.zeros_like(racc)
     iacc[...] = jnp.zeros_like(iacc)
 
@@ -171,9 +180,6 @@
             w1_copy(r, d).wait()
         for d in range(1, S):
             w2_copy(r, d, g).start()
-
-    def crim_use(up):
-        pass
 
     def early():
         w_mine(w2_go)
@@ -219,7 +225,8 @@
                 total += lax.dot_general(
                     left, vall[1, :, z * HW : (z + 1) * HW], (((1,), (1,)), ((), ())), preferred_element_type=F32
                 )
-            fflat[pl.ds(pl.multiple_of(step * 3 * fb, 8), 3 * fb), :] = total
+            for b in range(3):
+                fflat[rows(9 * a + 3 * b + c, fb), :] = total[b * fb : (b + 1) * fb]
             return 0
 
         lax.fori_loop(0, 9, body, 0)
@@ -237,25 +244,36 @@
     tile = 2 * W if H % 2 == 0 else W
     per_plane = HW // tile
 
-    def conv(weights, source, acc, size, forward):
-        def body(step, _):
-            z, q = step // per_plane, step % per_plane
-            lanes = pl.ds(pl.multiple_of(step * tile, W), tile)
-            right = source[:, :, lanes].reshape(3 * source.shape[1], tile)
-            product = jnp.dot(weights[...], right, preferred_element_type=F32)
-            for a in range(3):
-                plane = z + 2 - a if forward else z + a
-                for b in range(3):
-                    off = 2 - b if forward else b
-                    spot = pl.ds(pl.multiple_of(q * tile + off * W, W), tile)
-                    k = 3 * a + b
-                    acc[plane, :, spot] += product[k * size : (k + 1) * size]
-            return 0
-
-        lax.fori_loop(0, D * per_plane, body, 0)
+    def conv(weights, pick, acc, size, forward, part):
+        for z in range(D):
+            rim = ([0] if z == 0 else []) + ([2] if z == D - 1 else [])
+            if forward:
+                rim = [2 - a for a in rim]
+            taps = {"all": [0, 1, 2], "rim": rim, "rest": [a for a in range(3) if a not in rim]}[part]
+            if not taps:
+                continue
+            low, high = min(taps), max(taps) + 1
+
+            def body(q, _):
+                lanes = pl.ds(pl.multiple_of(z * HW + q * tile, W), tile)
+                right = pick(lanes)
+                left = weights(pl.ds(low * 3 * size, (high - low) * 3 * size))
+                product = jnp.dot(left, right, preferred_element_type=F32)
+                for a in taps:
+                    plane = z + 2 - a if forward else z + a
+                    for b in range(3):
+                        off = 2 - b if forward else b
+                        spot = pl.ds(pl.multiple_of(q * tile + off * W, W), tile)
+                        k = 3 * (a - low) + b
+                        acc[plane, :, spot] += product[k * size : (k + 1) * size]
+                return 0
+
+            lax.fori_loop(0, per_plane, body, 0)
 
     def response():
-        conv(wfwd, vall, racc, fb, True)
+        conv(
+            lambda r: wfwd[r, :], lambda lanes: vall[:, :, lanes].reshape(3 * cb * n, tile), racc, fb, True, "all"
+        )
         both_ways(lambda up: rim_copy(0, up).start())
 
     def f2_copy(d):
@@ -295,9 +313,26 @@
                 def _():
                     w2_copy(r, d, g).wait_recv()
 
-        for c in range(3):
+        def turn(j, _):
             for g in range(gpc):
-                wst[g * W : (g + 1) * W, c * F : (c + 1) * F] = wsb[c * gpc + g].T
+                piece = jnp.concatenate([wsb[c * gpc + g, rows(j, fb), :] for c in range(3)], axis=0)
+                wst[j, g * W : (g + 1) * W, :] = piece.T
+            return 0
+
+        lax.fori_loop(0, n, turn, 0)
+
+    def conv_block(block, part="all"):
+        conv(
+            lambda r: wst[block, r, :],
+            lambda lanes: call[:, rows(block, fb), lanes].reshape(3 * fb, tile),
+            iacc, cb, False, part,
+        )
+
+    def conv_arrived(t, part="all"):
+        for direction in range(2):
+            @pl.when(zrecvs(direction, t))
+            def _():
+                conv_block(i - 1 - t if direction == 0 else i + 1 + t, part)
 
     def finish(which, out, acc, buf):
         @pl.when(s > 0)
@@ -318,32 +353,31 @@
             a1_copy(d).wait_recv()
             a2_copy(d).start()
 
-    work = [[response, kernel_swapped], [reduce_pair], [reduce_chips]]
-    at = {}
-    for k, items in enumerate(work):
-        at.setdefault(min(k, max(n - 2, 0)), []).extend(items)
+    kernel_swapped()
+    conv_block(i)
+    reduce_pair()
+    last = n - 2
     for t in range(n - 1):
         zwait(1, t)
-        if t + 1 < n - 1:
+        if t < last:
             zstart(1, t + 1)
         zshift(1, t)
-        if t < n - 2:
-            for item in at.get(t, []):
-                item()
-    for item in at.get(n - 2, []):
-        if item is not reduce_chips:
-            item()
-
-    conv(wst, call, iacc, cb, False)
+        if t < last:
+            conv_arrived(t)
+        if t == 0:
+            response()
+        if t == min(1, last):
+            reduce_chips()
+    conv_arrived(last, "rim")
     both_ways(lambda up: rim_copy(1, up).start())
-    reduce_chips()
+    conv_arrived(last, "rest")
     finish(0, resp, racc, rbuf)
     gather_forward()
     finish(1, igrad, iacc, ibuf)
     for d in range(half):
         spot = fog.at[1 - e, (m - d + half) % half]
         remote(spot, spot, a2s.at[d], a2r.at[d], {"sp": sib}).wait_recv()
-    fout[...] = fog[...]
+    fout[...] = fog.reshape(2 * half * R, n * cb)[0 : 27 * fb, :]
 
     for which in range(2):
         for t in range(n - 1):
@@ -367,16 +401,12 @@
     fb = cotangent.shape[0]
     C, F = cb * n, fb * n
     cells = D * H * W
-    gpc = -(-9 * cb // W)
+    gpc = -(-9 // (W // cb))
     G = 3 * gpc
     half = S // 2
     R = -(-27 * fb // (S * 16)) * 16
     factor = 1.0 / math.sqrt(cells * S)
-    taps = filters.reshape(fb, 9, 3, C)
-    wfwd = jnp.transpose(taps, (1, 0, 2, 3)).reshape(9 * fb, 3 * C)
-    sendw = jnp.transpose(taps.reshape(fb, 9, 3, n, cb), (3, 2, 0, 1, 4)).reshape(n, 3, fb, 9 * cb)
-    sendw = jnp.pad(sendw, ((0, 0), (0, 0), (0, 0), (0, gpc * W - 9 * cb)))
-    sendw = jnp.transpose(sendw.reshape(n, 3, fb, gpc, W), (0, 1, 3, 2, 4)).reshape(n, G, fb, W)
+    filt = jnp.transpose(filters, (1, 2, 3, 0, 4)).reshape(27, fb, C)
     dma = pltpu.SemaphoreType.DMA
     spec = pl.BlockSpec(memory_space=pltpu.VMEM)
     carried = -(-G // S)
@@ -386,9 +416,9 @@
         out_shape=(
             jax.ShapeDtypeStruct((fb, cells), BF),
             jax.ShapeDtypeStruct((cb, cells), BF),
-            jax.ShapeDtypeStruct((2, half, R, C), BF),
+            jax.ShapeDtypeStruct((27 * fb, C), BF),
         ),
-        in_specs=[spec] * 4,
+        in_specs=[spec] * 3,
         out_specs=(spec,) * 3,
         scratch_shapes=[
             pltpu.VMEM((3, C, cells), BF),
@@ -399,8 +429,10 @@
             pltpu.VMEM((D + 2, cb, pads), F32),
             pltpu.VMEM((2, fb, H * W), F32),
             pltpu.VMEM((2, cb, H * W), F32),
+            pltpu.VMEM((9 * fb, 3 * C), BF),
+            pltpu.VMEM((carried, n, fb, W), BF),
             pltpu.VMEM((G, F, W), BF),
-            pltpu.VMEM((gpc * W, 3 * F), BF),
+            pltpu.VMEM((n, gpc * W, 3 * fb), BF),
             pltpu.VMEM((2, half, R, C), F32),
             pltpu.VMEM((half, R, C), F32),
             pltpu.VMEM((half - 1, R, C), F32),
@@ -427,12 +459,11 @@
         compiler_params=pltpu.CompilerParams(
             collective_id=0, has_side_effects=True, vmem_limit_bytes=50 * 2**20
         ),
-    )(volume.reshape(cb, cells), cotangent.reshape(fb, cells), wfwd, sendw)
-    fgrad = fgrad.reshape(S * R, C)[: 27 * fb].reshape(3, 3, 3, fb, C)
+    )(volume.reshape(cb, cells), cotangent.reshape(fb, cells), filt)
     return (
         resp.reshape(fb, D, H, W),
         igrad.reshape(cb, D, H, W),
-        jnp.transpose(fgrad, (3, 0, 2, 1, 4)),
+        jnp.transpose(fgrad.reshape(3, 3, 3, fb, C), (3, 0, 1, 2, 4)),
     )
 
 

time: 80.3 us -> 69 us (0.86)
  local copies, waits for them, and re-layouts: 14.4 us -> 3.72 us
    another operation x3 -> x0, local copies, waits for them, and re-layouts: 6.54 us -> none  [the longest x2 5.37 us: local(): taps.reshape(fb, 9, 3, n, cb)]
    concatenate x2 -> x0, local copies, waits for them, and re-layouts: 3.16 us -> none
    unnamed x8 -> x5, local copies, waits for them, and re-layouts: 2.82 us -> 2.51 us
where the time goes in v2:
time: 69 us; the launch traced here: 68.9 us
  Pallas kernels  64.5 us (93%)
  local copies, waits for them, and re-layouts  3.72 us (5%)
    pallas_call x1, Pallas kernels, local(): pl.pallas_call(functools.partial(kernel, n, S, D, H, W, gpc, factor), out...  64.5 us
    unnamed x5, local copies, waits for them, and re-layouts  2.51 us

profile of v2, /device:TPU:1, one launch (start us, length us, event | category | flops | bytes accessed | tf_op | source)
XLA Modules:
  0.0 68.9 jit_solution(18321083681527368425)
XLA Ops:
  0.6 0.0 copy-start
  0.6 1.2 %copy_bitcast_fusion = (bf16[64,2048]{1,0:T(8,128)(2,1)S(1)}, bf16[64,2048]{1,0:T(8,128)(2,1)S(1)}) fusion(bf16[8,8,16,128]{3,2,1,0:T(8,128)(2,1)} %bitcast.26, bf16[8,8,16,128]{3,2,1,0:T(8,128)(2,1)} %bitcast.27), kind=kLoop, calls=%fused_computation | loop fusion | bytes 1048576 | tf_op jit(solution)/shard_map/reshape | solution.py:462
  1.9 0.1 copy-done
  2.0 64.5 %shard_map.58 = (bf16[64,2048]{1,0:T(8,128)(2,1)S(1)}, bf16[64,2048]{1,0:T(8,128)(2,1)S(1)}, bf16[1728,256]{1,0:T(8,128)(2,1)S(1)}) custom-call(bf16[64,2048]{1,0:T(8,128)(2,1)S(1)} %get-tuple-element.10.vol, bf16[64,2048]{1,0:T(8,128)(2,1)S(1)} %get-tuple-element.9.cot, bf16[27,64,256]{2,1,0:T(8,128)(2,1)S(1)} %bitcast.21), custom_call_target="tpu_custom_call" | custom-call | tf_op jit(solution)/shard_map/pallas_call | solution.py:414
  66.5 0.7 %copy.8 = bf16[8,8,16,128]{3,2,1,0:T(8,128)(2,1)} copy(bf16[8,8,16,128]{3,1,2,0:T(8,128)(2,1)S(1)} %bitcast.23) | data formatting | bytes 524288
  67.2 0.7 %copy.9 = bf16[8,8,16,128]{3,2,1,0:T(8,128)(2,1)} copy(bf16[8,8,16,128]{3,1,2,0:T(8,128)(2,1)S(1)} %bitcast.22) | data formatting | bytes 524288
  68.0 0.9 %copy.13 = bf16[64,3,3,3,256]{4,0,3,2,1:T(8,128)(2,1)} copy(bf16[64,3,3,3,256]{4,0,3,2,1:T(8,128)(2,1)S(1)} %bitcast.20) | data formatting | bytes 1769472
Async XLA Ops:
  0.6 1.3 %copy-start = (bf16[64,3,3,3,256]{4,0,3,2,1:T(8,128)(2,1)S(1)}, bf16[64,3,3,3,256]{4,0,3,2,1:T(8,128)(2,1)}, u32[]{:S(2)}) copy-start(bf16[64,3,3,3,256]{4,0,3,2,1:T(8,128)(2,1)} %param.4) | copy-start | bytes 2654212

commit v3 on v2

--- a/solution.py
+++ b/solution.py
@@ -13,19 +13,22 @@
 
 
 def shifts(x, width):
-    wide = x.astype(F32)
-    lane = lax.broadcasted_iota(jnp.int32, x.shape, 1) % width
-    before = jnp.where(lane == 0, 0.0, pltpu.roll(wide, 1, 1)).astype(BF)
-    after = jnp.where(lane == width - 1, 0.0, pltpu.roll(wide, x.shape[1] - 1, 1)).astype(BF)
-    return before, after
+    lane = lax.broadcasted_iota(jnp.int32, (x.shape[0], width), 1)
+    first, last = lane == 0, lane == width - 1
+    before, after = [], []
+    for k in range(x.shape[1] // width):
+        wide = x[:, k * width : (k + 1) * width].astype(F32)
+        before.append(jnp.where(first, 0.0, pltpu.roll(wide, 1, 1)).astype(BF))
+        after.append(jnp.where(last, 0.0, pltpu.roll(wide, width - 1, 1)).astype(BF))
+    return jnp.concatenate(before, axis=1), jnp.concatenate(after, axis=1)
 
 
 def kernel(
     n, S, D, H, W, gpc, factor,
     vol, cot, filt,
     resp, igrad, fout,
-    vall, call, edge, crim, racc, iacc, rbuf, ibuf, wfwd, swb, wsb, wst, fpart, rs1, rs2, fog,
-    zs, zr, ws1, wr1, ws2, wr2, cs, cr, rims, rimr, f1s, f1r, f2s, f2r, a1s, a1r, a2s, a2r,
+    vall, call, edge, crim, racc, iacc, rbuf, ibuf, wfwd, swb, wsb, wst, wl, lv, lc, lrim, lcall, fpart, rs1, rs2, fog,
+    zs, zr, ws1, wr1, ws2, wr2, cs, cr, rims, rimr, f1s, f1r, f2s, f2r, a1s, a1r, a2s, a2r, ls, lr,
 ):
     i, s = lax.axis_index("ch"), lax.axis_index("sp")
     cb, cells = vol.shape
@@ -54,13 +57,11 @@
         return pl.ds(pl.multiple_of(j * size, size), size)
 
     def zcopy(which, direction, t):
-        buf, own = ((vall, vol), (call, cot))[which]
-        size = own.shape[0]
+        land, own = ((lv, vol), (lc, cot))[which]
         block = i - t if direction == 0 else i + t
-        spot = buf.at[1, rows(block, size), :]
-        src = own if t == 0 else spot
+        src = own if t == 0 else land.at[block]
         to = i + 1 if direction == 0 else i - 1
-        return remote(src, spot, zs.at[which, direction, t], zr.at[which, direction, t], {"ch": to})
+        return remote(src, land.at[block], zs.at[which, direction, t], zr.at[which, direction, t], {"ch": to})
 
     def zsends(direction, t):
         return (i < n - 1) & (i - t >= 0) if direction == 0 else (i > 0) & (i + t <= n - 1)
@@ -75,25 +76,25 @@
                 zcopy(which, direction, t).start()
 
     def zwait(which, t):
-        buf, own = ((vall, vol), (call, cot))[which]
-        size = own.shape[0]
+        land = (lv, lc)[which]
         for direction in range(2):
             @pl.when(zrecvs(direction, t))
             def _():
-                block = i - 1 - t if direction == 0 else i + 1 + t
-                spot = buf.at[1, rows(block, size), :]
+                spot = land.at[i - 1 - t if direction == 0 else i + 1 + t]
                 remote(spot, spot, zs.at[which, direction, t], zr.at[which, direction, t], {"ch": (i + 1) % n}).wait_recv()
 
     def zshift(which, t):
-        buf, own = ((vall, vol), (call, cot))[which]
-        size = own.shape[0]
+        land, buf = ((lv, vall), (lc, call))[which]
+        size = land.shape[1]
         for direction in range(2):
             @pl.when(zrecvs(direction, t))
             def _():
                 block = i - 1 - t if direction == 0 else i + 1 + t
                 place = rows(block, size)
-                before, after = shifts(buf[1, place, :], W)
+                x = land[block]
+                before, after = shifts(x, W)
                 buf[0, place, :] = before if which == 0 else after
+                buf[1, place, :] = x
                 buf[2, place, :] = after if which == 0 else before
 
     def zfinish(which, t):
@@ -165,6 +166,14 @@
     call[0, rows(i, fb), :] = after
     call[1, rows(i, fb), :] = x
     call[2, rows(i, fb), :] = before
+    ends = (i == 0) | (i == n - 1)
+    far = jnp.where(i == 0, n - 1, 0)
+
+    @pl.when(ends)
+    def _():
+        for c in range(3):
+            call[c, rows(far, fb), :] = jnp.zeros((fb, cells), BF)
+
     edge[...] = jnp.zeros_like(edge)
     for c, part in enumerate((after, x, before)):
         for z in range(D):
@@ -214,22 +223,20 @@
     R = fpart.shape[2]
 
     def fgrad():
-        def body(step, _):
-            a, c = step // 3, step % 3
-            total = jnp.zeros((3 * fb, n * cb), F32)
+        def body(a, _):
+            total = jnp.zeros((9 * fb, n * cb), F32)
             for z in range(D):
                 plane = z + 2 - a
                 left = jnp.concatenate(
-                    [edge[c, plane, :, (2 - b) * W : (2 - b) * W + HW] for b in range(3)], axis=0
+                    [edge[c, plane, :, (2 - b) * W : (2 - b) * W + HW] for b in range(3) for c in range(3)], axis=0
                 )
                 total += lax.dot_general(
                     left, vall[1, :, z * HW : (z + 1) * HW], (((1,), (1,)), ((), ())), preferred_element_type=F32
                 )
-            for b in range(3):
-                fflat[rows(9 * a + 3 * b + c, fb), :] = total[b * fb : (b + 1) * fb]
+            fflat[rows(a, 9 * fb), :] = total
             return 0
 
-        lax.fori_loop(0, 9, body, 0)
+        lax.fori_loop(0, 3, body, 0)
 
     fflat = fpart.reshape(2 * half * R, n * cb)
     if 27 * fb < 2 * half * R:
@@ -241,7 +248,7 @@
 
     f1_copy().start()
 
-    tile = 2 * W if H % 2 == 0 else W
+    tile = 4 * W if H % 4 == 0 else W
     per_plane = HW // tile
 
     def conv(weights, pick, acc, size, forward, part):
@@ -313,26 +320,52 @@
                 def _():
                     w2_copy(r, d, g).wait_recv()
 
-        def turn(j, _):
-            for g in range(gpc):
-                piece = jnp.concatenate([wsb[c * gpc + g, rows(j, fb), :] for c in range(3)], axis=0)
-                wst[j, g * W : (g + 1) * W, :] = piece.T
-            return 0
-
-        lax.fori_loop(0, n, turn, 0)
-
-    def conv_block(block, part="all"):
+        for g in range(gpc):
+            for c in range(3):
+                wst[g * W : (g + 1) * W, c * F : (c + 1) * F] = wsb[c * gpc + g].T
+            piece = jnp.concatenate([wsb[c * gpc + g, rows(far, fb), :] for c in range(3)], axis=0)
+            wl[g * W : (g + 1) * W, :] = piece.T
+
+    def most_blocks():
         conv(
-            lambda r: wst[block, r, :],
-            lambda lanes: call[:, rows(block, fb), lanes].reshape(3 * fb, tile),
-            iacc, cb, False, part,
+            lambda r: wst[r, :], lambda lanes: call[:, :, lanes].reshape(3 * F, tile), iacc, cb, False, "all"
         )
-
-    def conv_arrived(t, part="all"):
-        for direction in range(2):
-            @pl.when(zrecvs(direction, t))
-            def _():
-                conv_block(i - 1 - t if direction == 0 else i + 1 + t, part)
+        both_ways(lambda up: rim_copy(1, up).start())
+
+    def far_rim(up):
+        plane = lc.at[far, :, (D - 1) * HW : D * HW] if up else lc.at[far, :, 0:HW]
+        k = 0 if up else 1
+        return remote(plane, lrim.at[k], ls.at[k], lr.at[k], {"sp": s + 1 if up else s - 1})
+
+    def far_use(k):
+        remote(lrim.at[k], lrim.at[k], ls.at[k], lr.at[k], {"sp": (s + 1) % S}).wait_recv()
+        x = lrim[k]
+        before, after = shifts(x, W)
+        right = jnp.concatenate([after, x, before], axis=0)
+        a = 2 if k == 0 else 0
+        product = jnp.dot(wl[3 * a * cb : 3 * (a + 1) * cb, :], right, preferred_element_type=F32)
+        plane = 1 if k == 0 else D
+        for b in range(3):
+            iacc[plane, :, b * W : b * W + HW] += product[b * cb : (b + 1) * cb]
+
+    def far_block():
+        both_ways(lambda up: far_rim(up).start())
+        x = lc[far]
+        before, after = shifts(x, W)
+        lcall[0:fb, :] = after
+        lcall[fb : 2 * fb, :] = x
+        lcall[2 * fb :, :] = before
+        conv(lambda r: wl[r, :], lambda lanes: lcall[:, lanes], iacc, cb, False, "rest")
+
+        @pl.when(s > 0)
+        def _():
+            far_use(0)
+
+        @pl.when(s < S - 1)
+        def _():
+            far_use(1)
+
+        both_ways(lambda up: far_rim(up).wait_send())
 
     def finish(which, out, acc, buf):
         @pl.when(s > 0)
@@ -353,26 +386,25 @@
             a1_copy(d).wait_recv()
             a2_copy(d).start()
 
-    kernel_swapped()
-    conv_block(i)
-    reduce_pair()
     last = n - 2
-    for t in range(n - 1):
+    for t in range(last):
         zwait(1, t)
-        if t < last:
-            zstart(1, t + 1)
-        zshift(1, t)
-        if t < last:
-            conv_arrived(t)
+        zstart(1, t + 1)
         if t == 0:
             response()
-        if t == min(1, last):
-            reduce_chips()
-    conv_arrived(last, "rim")
-    both_ways(lambda up: rim_copy(1, up).start())
-    conv_arrived(last, "rest")
+            reduce_pair()
+        zshift(1, t)
+    kernel_swapped()
+    most_blocks()
+    reduce_chips()
     finish(0, resp, racc, rbuf)
     gather_forward()
+    zwait(1, last)
+
+    @pl.when(ends)
+    def _():
+        far_block()
+
     finish(1, igrad, iacc, ibuf)
     for d in range(half):
         spot = fog.at[1 - e, (m - d + half) % half]
@@ -432,7 +464,12 @@
             pltpu.VMEM((9 * fb, 3 * C), BF),
             pltpu.VMEM((carried, n, fb, W), BF),
             pltpu.VMEM((G, F, W), BF),
-            pltpu.VMEM((n, gpc * W, 3 * fb), BF),
+            pltpu.VMEM((gpc * W, 3 * F), BF),
+            pltpu.VMEM((gpc * W, 3 * fb), BF),
+            pltpu.VMEM((n, cb, cells), BF),
+            pltpu.VMEM((n, fb, cells), BF),
+            pltpu.VMEM((2, fb, H * W), BF),
+            pltpu.VMEM((3 * fb, cells), BF),
             pltpu.VMEM((2, half, R, C), F32),
             pltpu.VMEM((half, R, C), F32),
             pltpu.VMEM((half - 1, R, C), F32),
@@ -455,6 +492,8 @@
             dma((half - 1,)),
             dma((half,)),
             dma((half,)),
+            dma((2,)),
+            dma((2,)),
         ],
         compiler_params=pltpu.CompilerParams(
             collective_id=0, has_side_effects=True, vmem_limit_bytes=50 * 2**20

time: 69 us -> 73.2 us (1.061)
  Pallas kernels: 64.5 us -> 68.7 us
    pallas_call x1, Pallas kernels: 64.5 us -> 68.7 us  [local(): pl.pallas_call(functools.partial(kernel, n, S, D, H, W, gpc, factor), out...]
where the time goes in v3:
time: 73.2 us; the launch traced here: 73.1 us
  Pallas kernels  68.7 us (94%)
  local copies, waits for them, and re-layouts  3.72 us (5%)
    pallas_call x1, Pallas kernels, local(): pl.pallas_call(functools.partial(kernel, n, S, D, H, W, gpc, factor), out...  68.7 us
    unnamed x5, local copies, waits for them, and re-layouts  2.51 us

profile of v3, /device:TPU:1, one launch (start us, length us, event | category | flops | bytes accessed | tf_op | source)
XLA Modules:
  0.0 73.1 jit_solution(10814582528289018024)
XLA Ops:
  0.6 0.0 copy-start
  0.6 1.2 %copy_bitcast_fusion = (bf16[64,2048]{1,0:T(8,128)(2,1)S(1)}, bf16[64,2048]{1,0:T(8,128)(2,1)S(1)}) fusion(bf16[8,8,16,128]{3,2,1,0:T(8,128)(2,1)} %bitcast.26, bf16[8,8,16,128]{3,2,1,0:T(8,128)(2,1)} %bitcast.27), kind=kLoop, calls=%fused_computation | loop fusion | bytes 1048576 | tf_op jit(solution)/shard_map/reshape | solution.py:501
  1.9 0.1 copy-done
  2.0 68.7 %shard_map.58 = (bf16[64,2048]{1,0:T(8,128)(2,1)S(1)}, bf16[64,2048]{1,0:T(8,128)(2,1)S(1)}, bf16[1728,256]{1,0:T(8,128)(2,1)S(1)}) custom-call(bf16[64,2048]{1,0:T(8,128)(2,1)S(1)} %get-tuple-element.10.vol, bf16[64,2048]{1,0:T(8,128)(2,1)S(1)} %get-tuple-element.9.cot, bf16[27,64,256]{2,1,0:T(8,128)(2,1)S(1)} %bitcast.21), custom_call_target="tpu_custom_call" | custom-call | tf_op jit(solution)/shard_map/pallas_call | solution.py:446
  70.7 0.7 %copy.8 = bf16[8,8,16,128]{3,2,1,0:T(8,128)(2,1)} copy(bf16[8,8,16,128]{3,1,2,0:T(8,128)(2,1)S(1)} %bitcast.23) | data formatting | bytes 524288
  71.4 0.7 %copy.9 = bf16[8,8,16,128]{3,2,1,0:T(8,128)(2,1)} copy(bf16[8,8,16,128]{3,1,2,0:T(8,128)(2,1)S(1)} %bitcast.22) | data formatting | bytes 524288
  72.1 0.9 %copy.13 = bf16[64,3,3,3,256]{4,0,3,2,1:T(8,128)(2,1)} copy(bf16[64,3,3,3,256]{4,0,3,2,1:T(8,128)(2,1)S(1)} %bitcast.20) | data formatting | bytes 1769472
Async XLA Ops:
  0.6 1.3 %copy-start = (bf16[64,3,3,3,256]{4,0,3,2,1:T(8,128)(2,1)S(1)}, bf16[64,3,3,3,256]{4,0,3,2,1:T(8,128)(2,1)}, u32[]{:S(2)}) copy-start(bf16[64,3,3,3,256]{4,0,3,2,1:T(8,128)(2,1)} %param.4) | copy-start | bytes 2654212

commit v4 on v3

--- a/solution.py
+++ b/solution.py
@@ -28,7 +28,7 @@
     vol, cot, filt,
     resp, igrad, fout,
     vall, call, edge, crim, racc, iacc, rbuf, ibuf, wfwd, swb, wsb, wst, wl, lv, lc, lrim, lcall, fpart, rs1, rs2, fog,
-    zs, zr, ws1, wr1, ws2, wr2, cs, cr, rims, rimr, f1s, f1r, f2s, f2r, a1s, a1r, a2s, a2r, ls, lr,
+    zs, zr, ws1, wr1, ws2, wr2, cs, cr, rims, rimr, f1s, f1r, f2s, f2r, a1s, a1r, a2s, a2r, ls, lr, ws3, wr3,
 ):
     i, s = lax.axis_index("ch"), lax.axis_index("sp")
     cb, cells = vol.shape
@@ -132,7 +132,19 @@
         )
 
     def w2_copy(r, d, g):
-        return remote(wsb.at[g], wsb.at[g], ws2.at[r, d - 1], wr2.at[r, d - 1], {"sp": (s + d) % S})
+        to = ((m + d) % half) * 2 + e
+        return remote(wsb.at[g], wsb.at[g], ws2.at[r, d - 1], wr2.at[r, d - 1], {"sp": to})
+
+    def w3_copy(r, d, g):
+        return remote(wsb.at[g], wsb.at[g], ws3.at[r, d], wr3.at[r, d], {"sp": sib})
+
+    def w_from(d, core, act):
+        for r in range(carried):
+            g = ((m - d + half) % half) * 2 + core + r * S
+
+            @pl.when(g < G)
+            def _():
+                act(r, d, g)
 
     def w_mine(act):
         for r in range(carried):
@@ -187,12 +199,11 @@
     def w2_go(r, g):
         for d in range(1, n):
             w1_copy(r, d).wait()
-        for d in range(1, S):
+        for d in range(1, half):
             w2_copy(r, d, g).start()
+        w3_copy(r, 0, g).start()
 
     def early():
-        w_mine(w2_go)
-
         @pl.when(s > 0)
         def _():
             remote(crim.at[0], crim.at[0], cs.at[0], cr.at[0], {"sp": (s + 1) % S}).wait_recv()
@@ -209,44 +220,100 @@
             for c, part in enumerate((after, x, before)):
                 edge[c, D + 1, :, W : W + HW] = part
 
-    for t in range(n - 1):
-        zwait(0, t)
-        if t + 1 < n - 1:
-            zstart(0, t + 1)
-        if t + 1 >= n - 2:
-            if t + 1 == max(n - 2, 1):
-                zstart(1, 0)
-        zshift(0, t)
-        if t == 0:
-            early()
-
-    R = fpart.shape[2]
-
-    def fgrad():
+    R, Ch = fpart.shape[3], fpart.shape[4]
+    pair = i // (n // 2)
+
+    def fgrad(h):
+        flat = fpart.at[h].reshape(2 * half * R, Ch)
+        if 27 * fb < 2 * half * R:
+            flat[27 * fb :, :] = jnp.zeros((2 * half * R - 27 * fb, Ch), F32)
+        place = rows(pair if h == 0 else 1 - pair, Ch)
+
         def body(a, _):
-            total = jnp.zeros((9 * fb, n * cb), F32)
+            total = jnp.zeros((9 * fb, Ch), F32)
             for z in range(D):
                 plane = z + 2 - a
                 left = jnp.concatenate(
                     [edge[c, plane, :, (2 - b) * W : (2 - b) * W + HW] for b in range(3) for c in range(3)], axis=0
                 )
                 total += lax.dot_general(
-                    left, vall[1, :, z * HW : (z + 1) * HW], (((1,), (1,)), ((), ())), preferred_element_type=F32
+                    left, vall[1, place, z * HW : (z + 1) * HW], (((1,), (1,)), ((), ())), preferred_element_type=F32
                 )
-            fflat[rows(a, 9 * fb), :] = total
+            flat[rows(a, 9 * fb), :] = total
             return 0
 
         lax.fori_loop(0, 3, body, 0)
-
-    fflat = fpart.reshape(2 * half * R, n * cb)
-    if 27 * fb < 2 * half * R:
-        fflat[27 * fb :, :] = jnp.zeros((2 * half * R - 27 * fb, n * cb), F32)
-    fgrad()
-
-    def f1_copy():
-        return remote(fpart.at[1 - e], rs1, f1s, f1r, {"sp": sib})
-
-    f1_copy().start()
+        f1_copy(h).start()
+
+    def f1_copy(h):
+        return remote(fpart.at[h, 1 - e], rs1.at[h], f1s.at[h], f1r.at[h], {"sp": sib})
+
+    def f2_copy(h, d):
+        to = ((m + d) % half) * 2 + e
+        src = fpart.at[h, e, (m + d) % half]
+        return remote(src, rs2.at[h, d - 1], f2s.at[h, d - 1], f2r.at[h, d - 1], {"sp": to})
+
+    def reduce_pair(h):
+        f1_copy(h).wait()
+        fpart[h, e] = fpart[h, e] + rs1[h]
+        for d in range(1, half):
+            f2_copy(h, d).start()
+
+    def a1_copy(h, d):
+        spot = fog.at[h, e, m]
+        return remote(spot, spot, a1s.at[h, d - 1], a1r.at[h, d - 1], {"sp": ((m + d) % half) * 2 + e})
+
+    def a2_copy(h, d):
+        spot = fog.at[h, e, (m - d + half) % half]
+        return remote(spot, spot, a2s.at[h, d], a2r.at[h, d], {"sp": sib})
+
+    def reduce_chips(h):
+        total = fpart[h, e, m]
+        for d in range(1, half):
+            f2_copy(h, d).wait()
+            total = total + rs2[h, d - 1]
+        fog[h, e, m] = (total * factor).astype(BF)
+        for d in range(1, half):
+            a1_copy(h, d).start()
+        a2_copy(h, 0).start()
+
+    def gather_forward(h):
+        for d in range(1, half):
+            a1_copy(h, d).wait_recv()
+            a2_copy(h, d).start()
+
+    def gather_end(h):
+        for d in range(half):
+            spot = fog.at[h, 1 - e, (m - d + half) % half]
+            remote(spot, spot, a2s.at[h, d], a2r.at[h, d], {"sp": sib}).wait_recv()
+        lanes = pl.ds(pl.multiple_of((pair if h == 0 else 1 - pair) * Ch, Ch), Ch)
+        fout[:, lanes] = fog.at[h].reshape(2 * half * R, Ch)[0 : 27 * fb, :]
+
+    def w3_go():
+        def pass_on(r, d, g):
+            w2_copy(r, d, g).wait_recv()
+            w3_copy(r, d, g).start()
+
+        for d in range(1, half):
+            w_from(d, e, pass_on)
+
+    own_half = max(n // 2 - 2, 0)
+    for t in range(n - 1):
+        zwait(0, t)
+        if t + 1 < n - 1:
+            zstart(0, t + 1)
+        if t + 1 == max(n - 2, 1):
+            zstart(1, 0)
+        zshift(0, t)
+        if t == 0:
+            early()
+        if t == own_half:
+            fgrad(0)
+            w_mine(w2_go)
+        if t == own_half + 1:
+            reduce_pair(0)
+    fgrad(1)
+    w3_go()
 
     tile = 4 * W if H % 4 == 0 else W
     per_plane = HW // tile
@@ -283,42 +350,9 @@
         )
         both_ways(lambda up: rim_copy(0, up).start())
 
-    def f2_copy(d):
-        to = ((m + d) % half) * 2 + e
-        return remote(fpart.at[e, (m + d) % half], rs2.at[d - 1], f2s.at[d - 1], f2r.at[d - 1], {"sp": to})
-
-    def reduce_pair():
-        f1_copy().wait()
-        fpart[e] = fpart[e] + rs1[...]
-        for d in range(1, half):
-            f2_copy(d).start()
-
-    def a1_copy(d):
-        spot = fog.at[e, m]
-        return remote(spot, spot, a1s.at[d - 1], a1r.at[d - 1], {"sp": ((m + d) % half) * 2 + e})
-
-    def a2_copy(d):
-        spot = fog.at[e, (m - d + half) % half]
-        return remote(spot, spot, a2s.at[d], a2r.at[d], {"sp": sib})
-
-    def reduce_chips():
-        total = fpart[e, m]
-        for d in range(1, half):
-            f2_copy(d).wait()
-            total = total + rs2[d - 1]
-        fog[e, m] = (total * factor).astype(BF)
-        for d in range(1, half):
-            a1_copy(d).start()
-        a2_copy(0).start()
-
     def kernel_swapped():
-        for r in range(carried):
-            for d in range(1, S):
-                g = (s - d + S) % S + r * S
-
-                @pl.when(g < G)
-                def _():
-                    w2_copy(r, d, g).wait_recv()
+        for d in range(half):
+            w_from(d, 1 - e, lambda r, d, g: w3_copy(r, d, g).wait_recv())
 
         for g in range(gpc):
             for c in range(3):
@@ -381,24 +415,21 @@
         for z in range(D):
             out[:, z * HW : (z + 1) * HW] = acc[z + 1, :, W : W + HW].astype(BF)
 
-    def gather_forward():
-        for d in range(1, half):
-            a1_copy(d).wait_recv()
-            a2_copy(d).start()
-
     last = n - 2
     for t in range(last):
         zwait(1, t)
         zstart(1, t + 1)
         if t == 0:
+            reduce_pair(1)
             response()
-            reduce_pair()
+            reduce_chips(0)
         zshift(1, t)
     kernel_swapped()
+    reduce_chips(1)
     most_blocks()
-    reduce_chips()
+    gather_forward(0)
+    gather_forward(1)
     finish(0, resp, racc, rbuf)
-    gather_forward()
     zwait(1, last)
 
     @pl.when(ends)
@@ -406,10 +437,8 @@
         far_block()
 
     finish(1, igrad, iacc, ibuf)
-    for d in range(half):
-        spot = fog.at[1 - e, (m - d + half) % half]
-        remote(spot, spot, a2s.at[d], a2r.at[d], {"sp": sib}).wait_recv()
-    fout[...] = fog.reshape(2 * half * R, n * cb)[0 : 27 * fb, :]
+    gather_end(0)
+    gather_end(1)
 
     for which in range(2):
         for t in range(n - 1):
@@ -418,14 +447,18 @@
     both_ways(lambda up: crim_copy(up).wait_send())
 
     def w2_end(r, g):
-        for d in range(1, S):
+        for d in range(1, half):
             w2_copy(r, d, g).wait_send()
+        w3_copy(r, 0, g).wait_send()
 
     w_mine(w2_end)
     for d in range(1, half):
-        a1_copy(d).wait_send()
-    for d in range(half):
-        a2_copy(d).wait_send()
+        w_from(d, e, lambda r, d, g: w3_copy(r, d, g).wait_send())
+    for h in range(2):
+        for d in range(1, half):
+            a1_copy(h, d).wait_send()
+        for d in range(half):
+            a2_copy(h, d).wait_send()
 
 
 def local(n, S, volume, filters, cotangent):
@@ -470,30 +503,32 @@
             pltpu.VMEM((n, fb, cells), BF),
             pltpu.VMEM((2, fb, H * W), BF),
             pltpu.VMEM((3 * fb, cells), BF),
-            pltpu.VMEM((2, half, R, C), F32),
-            pltpu.VMEM((half, R, C), F32),
-            pltpu.VMEM((half - 1, R, C), F32),
-            pltpu.VMEM((2, half, R, C), BF),
+            pltpu.VMEM((2, 2, half, R, C // 2), F32),
+            pltpu.VMEM((2, half, R, C // 2), F32),
+            pltpu.VMEM((2, half - 1, R, C // 2), F32),
+            pltpu.VMEM((2, 2, half, R, C // 2), BF),
             dma((2, 2, n - 1)),
             dma((2, 2, n - 1)),
             dma((carried, n - 1)),
             dma((carried, n - 1)),
-            dma((carried, S - 1)),
-            dma((carried, S - 1)),
+            dma((carried, half - 1)),
+            dma((carried, half - 1)),
             dma((2,)),
             dma((2,)),
             dma((2, 2)),
             dma((2, 2)),
-            dma,
-            dma,
-            dma((half - 1,)),
-            dma((half - 1,)),
-            dma((half - 1,)),
-            dma((half - 1,)),
-            dma((half,)),
-            dma((half,)),
             dma((2,)),
             dma((2,)),
+            dma((2, half - 1)),
+            dma((2, half - 1)),
+            dma((2, half - 1)),
+            dma((2, half - 1)),
+            dma((2, half)),
+            dma((2, half)),
+            dma((2,)),
+            dma((2,)),
+            dma((carried, half)),
+            dma((carried, half)),
         ],
         compiler_params=pltpu.CompilerParams(
             collective_id=0, has_side_effects=True, vmem_limit_bytes=50 * 2**20

time: 73.2 us -> 64.8 us (0.89)
  Pallas kernels: 68.7 us -> 60.2 us
    pallas_call x1, Pallas kernels: 68.7 us -> 60.2 us  [local(): pl.pallas_call(functools.partial(kernel, n, S, D, H, W, gpc, factor), out...]
where the time goes in v4:
time: 64.8 us; the launch traced here: 64.6 us
  Pallas kernels  60.2 us (93%)
  local copies, waits for them, and re-layouts  3.72 us (6%)
  between operations  0.65 us (1%)
    pallas_call x1, Pallas kernels, local(): pl.pallas_call(functools.partial(kernel, n, S, D, H, W, gpc, factor), out...  60.2 us
    unnamed x5, local copies, waits for them, and re-layouts  2.51 us

profile of v4, /device:TPU:1, one launch (start us, length us, event | category | flops | bytes accessed | tf_op | source)
XLA Modules:
  0.0 64.6 jit_solution(2457198203177587227)
XLA Ops:
  0.6 0.0 copy-start
  0.6 1.2 %copy_bitcast_fusion = (bf16[64,2048]{1,0:T(8,128)(2,1)S(1)}, bf16[64,2048]{1,0:T(8,128)(2,1)S(1)}) fusion(bf16[8,8,16,128]{3,2,1,0:T(8,128)(2,1)} %bitcast.26, bf16[8,8,16,128]{3,2,1,0:T(8,128)(2,1)} %bitcast.27), kind=kLoop, calls=%fused_computation | loop fusion | bytes 1048576 | tf_op jit(solution)/shard_map/reshape | solution.py:536
  1.9 0.1 copy-done
  2.0 60.2 %shard_map.58 = (bf16[64,2048]{1,0:T(8,128)(2,1)S(1)}, bf16[64,2048]{1,0:T(8,128)(2,1)S(1)}, bf16[1728,256]{1,0:T(8,128)(2,1)S(1)}) custom-call(bf16[64,2048]{1,0:T(8,128)(2,1)S(1)} %get-tuple-element.10.vol, bf16[64,2048]{1,0:T(8,128)(2,1)S(1)} %get-tuple-element.9.cot, bf16[27,64,256]{2,1,0:T(8,128)(2,1)S(1)} %bitcast.21), custom_call_target="tpu_custom_call" | custom-call | tf_op jit(solution)/shard_map/pallas_call | solution.py:479
  62.2 0.7 %copy.8 = bf16[8,8,16,128]{3,2,1,0:T(8,128)(2,1)} copy(bf16[8,8,16,128]{3,1,2,0:T(8,128)(2,1)S(1)} %bitcast.23) | data formatting | bytes 524288
  63.0 0.7 %copy.9 = bf16[8,8,16,128]{3,2,1,0:T(8,128)(2,1)} copy(bf16[8,8,16,128]{3,1,2,0:T(8,128)(2,1)S(1)} %bitcast.22) | data formatting | bytes 524288
  63.7 0.9 %copy.13 = bf16[64,3,3,3,256]{4,0,3,2,1:T(8,128)(2,1)} copy(bf16[64,3,3,3,256]{4,0,3,2,1:T(8,128)(2,1)S(1)} %bitcast.20) | data formatting | bytes 1769472
Async XLA Ops:
  0.6 1.3 %copy-start = (bf16[64,3,3,3,256]{4,0,3,2,1:T(8,128)(2,1)S(1)}, bf16[64,3,3,3,256]{4,0,3,2,1:T(8,128)(2,1)}, u32[]{:S(2)}) copy-start(bf16[64,3,3,3,256]{4,0,3,2,1:T(8,128)(2,1)} %param.4) | copy-start | bytes 2654212

commit v5 on v4

--- a/solution.py
+++ b/solution.py
@@ -56,12 +56,14 @@
     def rows(j, size):
         return pl.ds(pl.multiple_of(j * size, size), size)
 
-    def zcopy(which, direction, t):
+    def zcopy(which, direction, t, z):
         land, own = ((lv, vol), (lc, cot))[which]
         block = i - t if direction == 0 else i + t
-        src = own if t == 0 else land.at[block]
+        src = own.at[:, z * HW : (z + 1) * HW] if t == 0 else land.at[block, z]
         to = i + 1 if direction == 0 else i - 1
-        return remote(src, land.at[block], zs.at[which, direction, t], zr.at[which, direction, t], {"ch": to})
+        return remote(
+            src, land.at[block, z], zs.at[which, direction, t, z], zr.at[which, direction, t, z], {"ch": to}
+        )
 
     def zsends(direction, t):
         return (i < n - 1) & (i - t >= 0) if direction == 0 else (i > 0) & (i + t <= n - 1)
@@ -69,39 +71,44 @@
     def zrecvs(direction, t):
         return i - 1 - t >= 0 if direction == 0 else i + 1 + t <= n - 1
 
-    def zstart(which, t):
+    def zstart(which, t, z):
         for direction in range(2):
             @pl.when(zsends(direction, t))
             def _():
-                zcopy(which, direction, t).start()
-
-    def zwait(which, t):
+                zcopy(which, direction, t, z).start()
+
+    def zwait(which, t, z):
         land = (lv, lc)[which]
         for direction in range(2):
             @pl.when(zrecvs(direction, t))
             def _():
-                spot = land.at[i - 1 - t if direction == 0 else i + 1 + t]
-                remote(spot, spot, zs.at[which, direction, t], zr.at[which, direction, t], {"ch": (i + 1) % n}).wait_recv()
+                spot = land.at[i - 1 - t if direction == 0 else i + 1 + t, z]
+                remote(
+                    spot, spot, zs.at[which, direction, t, z], zr.at[which, direction, t, z], {"ch": (i + 1) % n}
+                ).wait_recv()
 
     def zshift(which, t):
         land, buf = ((lv, vall), (lc, call))[which]
-        size = land.shape[1]
+        size = land.shape[2]
         for direction in range(2):
             @pl.when(zrecvs(direction, t))
             def _():
                 block = i - 1 - t if direction == 0 else i + 1 + t
                 place = rows(block, size)
-                x = land[block]
-                before, after = shifts(x, W)
-                buf[0, place, :] = before if which == 0 else after
-                buf[1, place, :] = x
-                buf[2, place, :] = after if which == 0 else before
+                for z in range(D):
+                    x = land[block, z]
+                    before, after = shifts(x, W)
+                    cells_z = slice(z * HW, (z + 1) * HW)
+                    buf[0, place, cells_z] = before if which == 0 else after
+                    buf[1, place, cells_z] = x
+                    buf[2, place, cells_z] = after if which == 0 else before
 
     def zfinish(which, t):
         for direction in range(2):
             @pl.when(zsends(direction, t))
             def _():
-                zcopy(which, direction, t).wait_send()
+                for z in range(D):
+                    zcopy(which, direction, t, z).wait_send()
 
     def crim_copy(up):
         plane = cot.at[:, (D - 1) * HW : D * HW] if up else cot.at[:, 0:HW]
@@ -152,7 +159,8 @@
             def _():
                 act(r, s + r * S)
 
-    zstart(0, 0)
+    for z in range(D):
+        zstart(0, 0, z)
     both_ways(lambda up: crim_copy(up).start())
 
     tpg = W // cb
@@ -299,16 +307,26 @@
 
     own_half = max(n // 2 - 2, 0)
     for t in range(n - 1):
-        zwait(0, t)
-        if t + 1 < n - 1:
-            zstart(0, t + 1)
+        for z in range(D):
+            zwait(0, t, z)
+            if t + 1 < n - 1:
+                zstart(0, t + 1, z)
         if t + 1 == max(n - 2, 1):
-            zstart(1, 0)
+            for z in range(D):
+                zstart(1, 0, z)
+        if t == own_half + 1:
+            @pl.when(jnp.logical_not(ends))
+            def _():
+                fgrad(0)
+
         zshift(0, t)
         if t == 0:
             early()
         if t == own_half:
-            fgrad(0)
+            @pl.when(ends)
+            def _():
+                fgrad(0)
+
             w_mine(w2_go)
         if t == own_half + 1:
             reduce_pair(0)
@@ -318,8 +336,8 @@
     tile = 4 * W if H % 4 == 0 else W
     per_plane = HW // tile
 
-    def conv(weights, pick, acc, size, forward, part):
-        for z in range(D):
+    def conv(weights, pick, acc, size, forward, part, planes=range(D)):
+        for z in planes:
             rim = ([0] if z == 0 else []) + ([2] if z == D - 1 else [])
             if forward:
                 rim = [2 - a for a in rim]
@@ -367,7 +385,7 @@
         both_ways(lambda up: rim_copy(1, up).start())
 
     def far_rim(up):
-        plane = lc.at[far, :, (D - 1) * HW : D * HW] if up else lc.at[far, :, 0:HW]
+        plane = lc.at[far, D - 1 if up else 0]
         k = 0 if up else 1
         return remote(plane, lrim.at[k], ls.at[k], lr.at[k], {"sp": s + 1 if up else s - 1})
 
@@ -383,21 +401,31 @@
             iacc[plane, :, b * W : b * W + HW] += product[b * cb : (b + 1) * cb]
 
     def far_block():
-        both_ways(lambda up: far_rim(up).start())
-        x = lc[far]
-        before, after = shifts(x, W)
-        lcall[0:fb, :] = after
-        lcall[fb : 2 * fb, :] = x
-        lcall[2 * fb :, :] = before
-        conv(lambda r: wl[r, :], lambda lanes: lcall[:, lanes], iacc, cb, False, "rest")
+        for z in range(D):
+            zwait(1, last, z)
+            if z == 0:
+                @pl.when(s > 0)
+                def _():
+                    far_rim(False).start()
+
+            if z == D - 1:
+                @pl.when(s < S - 1)
+                def _():
+                    far_rim(True).start()
+
+            x = lc[far, z]
+            before, after = shifts(x, W)
+            for c, value in enumerate((after, x, before)):
+                lcall[c * fb : (c + 1) * fb, z * HW : (z + 1) * HW] = value
+            conv(lambda r: wl[r, :], lambda lanes: lcall[:, lanes], iacc, cb, False, "rest", [z])
+
+        @pl.when(s < S - 1)
+        def _():
+            far_use(1)
 
         @pl.when(s > 0)
         def _():
             far_use(0)
-
-        @pl.when(s < S - 1)
-        def _():
-            far_use(1)
 
         both_ways(lambda up: far_rim(up).wait_send())
 
@@ -416,13 +444,25 @@
             out[:, z * HW : (z + 1) * HW] = acc[z + 1, :, W : W + HW].astype(BF)
 
     last = n - 2
+    def forwards(t):
+        @pl.when(jnp.logical_not(ends))
+        def _():
+            for z in range(D):
+                zwait(1, t, z)
+                zstart(1, t + 1, z)
+
     for t in range(last):
-        zwait(1, t)
-        zstart(1, t + 1)
+        forwards(t)
         if t == 0:
             reduce_pair(1)
-            response()
-            reduce_chips(0)
+    response()
+    reduce_chips(0)
+    for t in range(last):
+        @pl.when(ends)
+        def _():
+            for z in range(D):
+                zwait(1, t, z)
+
         zshift(1, t)
     kernel_swapped()
     reduce_chips(1)
@@ -430,7 +470,6 @@
     gather_forward(0)
     gather_forward(1)
     finish(0, resp, racc, rbuf)
-    zwait(1, last)
 
     @pl.when(ends)
     def _():
@@ -499,16 +538,16 @@
             pltpu.VMEM((G, F, W), BF),
             pltpu.VMEM((gpc * W, 3 * F), BF),
             pltpu.VMEM((gpc * W, 3 * fb), BF),
-            pltpu.VMEM((n, cb, cells), BF),
-            pltpu.VMEM((n, fb, cells), BF),
+            pltpu.VMEM((n, D, cb, H * W), BF),
+            pltpu.VMEM((n, D, fb, H * W), BF),
             pltpu.VMEM((2, fb, H * W), BF),
             pltpu.VMEM((3 * fb, cells), BF),
             pltpu.VMEM((2, 2, half, R, C // 2), F32),
             pltpu.VMEM((2, half, R, C // 2), F32),
             pltpu.VMEM((2, half - 1, R, C // 2), F32),
             pltpu.VMEM((2, 2, half, R, C // 2), BF),
-            dma((2, 2, n - 1)),
-            dma((2, 2, n - 1)),
+            dma((2, 2, n - 1, D)),
+            dma((2, 2, n - 1, D)),
             dma((carried, n - 1)),
             dma((carried, n - 1)),
             dma((carried, half - 1)),

time: 64.8 us -> 62.4 us (0.963)
  Pallas kernels: 60.2 us -> 57.9 us
    pallas_call x1, Pallas kernels: 60.2 us -> 57.9 us  [local(): pl.pallas_call(functools.partial(kernel, n, S, D, H, W, gpc, factor), out...]
where the time goes in v5:
time: 62.4 us; the launch traced here: 62.3 us
  Pallas kernels  57.9 us (93%)
  local copies, waits for them, and re-layouts  3.72 us (6%)
  between operations  0.65 us (1%)
    pallas_call x1, Pallas kernels, local(): pl.pallas_call(functools.partial(kernel, n, S, D, H, W, gpc, factor), out...  57.9 us
    unnamed x5, local copies, waits for them, and re-layouts  2.51 us

profile of v5, /device:TPU:1, one launch (start us, length us, event | category | flops | bytes accessed | tf_op | source)
XLA Modules:
  0.0 62.3 jit_solution(1668369765459559405)
XLA Ops:
  0.6 0.0 copy-start
  0.6 1.2 %copy_bitcast_fusion = (bf16[64,2048]{1,0:T(8,128)(2,1)S(1)}, bf16[64,2048]{1,0:T(8,128)(2,1)S(1)}) fusion(bf16[8,8,16,128]{3,2,1,0:T(8,128)(2,1)} %bitcast.26, bf16[8,8,16,128]{3,2,1,0:T(8,128)(2,1)} %bitcast.27), kind=kLoop, calls=%fused_computation | loop fusion | bytes 1048576 | tf_op jit(solution)/shard_map/reshape | solution.py:575
  1.9 0.1 copy-done
  2.0 57.9 %shard_map.58 = (bf16[64,2048]{1,0:T(8,128)(2,1)S(1)}, bf16[64,2048]{1,0:T(8,128)(2,1)S(1)}, bf16[1728,256]{1,0:T(8,128)(2,1)S(1)}) custom-call(bf16[64,2048]{1,0:T(8,128)(2,1)S(1)} %get-tuple-element.10.vol, bf16[64,2048]{1,0:T(8,128)(2,1)S(1)} %get-tuple-element.9.cot, bf16[27,64,256]{2,1,0:T(8,128)(2,1)S(1)} %bitcast.21), custom_call_target="tpu_custom_call" | custom-call | tf_op jit(solution)/shard_map/pallas_call | solution.py:518
  59.9 0.7 %copy.8 = bf16[8,8,16,128]{3,2,1,0:T(8,128)(2,1)} copy(bf16[8,8,16,128]{3,1,2,0:T(8,128)(2,1)S(1)} %bitcast.23) | data formatting | bytes 524288
  60.6 0.7 %copy.9 = bf16[8,8,16,128]{3,2,1,0:T(8,128)(2,1)} copy(bf16[8,8,16,128]{3,1,2,0:T(8,128)(2,1)S(1)} %bitcast.22) | data formatting | bytes 524288
  61.4 0.9 %copy.13 = bf16[64,3,3,3,256]{4,0,3,2,1:T(8,128)(2,1)} copy(bf16[64,3,3,3,256]{4,0,3,2,1:T(8,128)(2,1)S(1)} %bitcast.20) | data formatting | bytes 1769472
Async XLA Ops:
  0.6 1.3 %copy-start = (bf16[64,3,3,3,256]{4,0,3,2,1:T(8,128)(2,1)S(1)}, bf16[64,3,3,3,256]{4,0,3,2,1:T(8,128)(2,1)}, u32[]{:S(2)}) copy-start(bf16[64,3,3,3,256]{4,0,3,2,1:T(8,128)(2,1)} %param.4) | copy-start | bytes 2654212

commit v6 on v5

--- a/solution.py
+++ b/solution.py
@@ -27,7 +27,7 @@
     n, S, D, H, W, gpc, factor,
     vol, cot, filt,
     resp, igrad, fout,
-    vall, call, edge, crim, racc, iacc, rbuf, ibuf, wfwd, swb, wsb, wst, wl, lv, lc, lrim, lcall, fpart, rs1, rs2, fog,
+    vall, call, edge, crim, racc, iacc, rbuf, wfwd, swb, wsb, wst, wl, lv, lc, lrim, lcall, fpart, rs1, rs2, fog,
     zs, zr, ws1, wr1, ws2, wr2, cs, cr, rims, rimr, f1s, f1r, f2s, f2r, a1s, a1r, a2s, a2r, ls, lr, ws3, wr3,
 ):
     i, s = lax.axis_index("ch"), lax.axis_index("sp")
@@ -98,7 +98,8 @@
                 for z in range(D):
                     x = land[block, z]
                     before, after = shifts(x, W)
-                    cells_z = slice(z * HW, (z + 1) * HW)
+                    at = z + which
+                    cells_z = slice(at * HW, (at + 1) * HW)
                     buf[0, place, cells_z] = before if which == 0 else after
                     buf[1, place, cells_z] = x
                     buf[2, place, cells_z] = after if which == 0 else before
@@ -115,11 +116,10 @@
         k = 0 if up else 1
         return remote(plane, crim.at[k], cs.at[k], cr.at[k], {"sp": s + 1 if up else s - 1})
 
-    def rim_copy(which, up):
-        acc, buf = ((racc, rbuf), (iacc, ibuf))[which]
+    def rim_copy(up):
         k = 0 if up else 1
-        src = acc.at[D + 1 if up else 0, :, W : W + HW]
-        return remote(src, buf.at[k], rims.at[which, k], rimr.at[which, k], {"sp": s + 1 if up else s - 1})
+        src = racc.at[D + 1 if up else 0, :, W : W + HW]
+        return remote(src, rbuf.at[k], rims.at[k], rimr.at[k], {"sp": s + 1 if up else s - 1})
 
     def both_ways(act):
         @pl.when(s < S - 1)
@@ -129,6 +129,40 @@
         @pl.when(s > 0)
         def _():
             act(False)
+
+    def block_at(direction, t):
+        return i - 1 - t if direction == 0 else i + 1 + t
+
+    def brim_copy(direction, t, up):
+        k = 0 if up else 1
+        block = block_at(direction, t)
+        return remote(
+            lc.at[block, D - 1 if up else 0], lrim.at[k, block], ls.at[k, direction, t], lr.at[k, direction, t],
+            {"sp": s + 1 if up else s - 1},
+        )
+
+    def brims(t, act):
+        for direction in range(2):
+            @pl.when(zrecvs(direction, t))
+            def _():
+                both_ways(lambda up: act(brim_copy(direction, t, up)))
+
+    def brim_wait(direction, t, k):
+        spot = lrim.at[k, block_at(direction, t)]
+        remote(spot, spot, ls.at[k, direction, t], lr.at[k, direction, t], {"sp": (s + 1) % S}).wait_recv()
+
+    def brims_use(t):
+        for direction in range(2):
+            for k in range(2):
+                @pl.when(zrecvs(direction, t) & ((s > 0) if k == 0 else (s < S - 1)))
+                def _():
+                    brim_wait(direction, t, k)
+                    block = block_at(direction, t)
+                    x = lrim[k, block]
+                    before, after = shifts(x, W)
+                    low = 0 if k == 0 else (D + 1) * HW
+                    for c, part in enumerate((after, x, before)):
+                        call[c, rows(block, fb), low : low + HW] = part
 
     carried = -(-G // S)
 
@@ -183,16 +217,17 @@
     vall[2, rows(i, cb), :] = after
     x = cot[...]
     before, after = shifts(x, W)
-    call[0, rows(i, fb), :] = after
-    call[1, rows(i, fb), :] = x
-    call[2, rows(i, fb), :] = before
+    for c, part in enumerate((after, x, before)):
+        call[c, rows(i, fb), HW : (D + 1) * HW] = part
+        call[c, :, 0:HW] = jnp.zeros((F, HW), BF)
+        call[c, :, (D + 1) * HW :] = jnp.zeros((F, HW), BF)
     ends = (i == 0) | (i == n - 1)
     far = jnp.where(i == 0, n - 1, 0)
 
     @pl.when(ends)
     def _():
         for c in range(3):
-            call[c, rows(far, fb), :] = jnp.zeros((fb, cells), BF)
+            call[c, rows(far, fb), HW : (D + 1) * HW] = jnp.zeros((fb, cells), BF)
 
     edge[...] = jnp.zeros_like(edge)
     for c, part in enumerate((after, x, before)):
@@ -219,6 +254,7 @@
             before, after = shifts(x, W)
             for c, part in enumerate((after, x, before)):
                 edge[c, 0, :, W : W + HW] = part
+                call[c, rows(i, fb), 0:HW] = part
 
         @pl.when(s < S - 1)
         def _():
@@ -227,6 +263,7 @@
             before, after = shifts(x, W)
             for c, part in enumerate((after, x, before)):
                 edge[c, D + 1, :, W : W + HW] = part
+                call[c, rows(i, fb), (D + 1) * HW :] = part
 
     R, Ch = fpart.shape[3], fpart.shape[4]
     pair = i // (n // 2)
@@ -336,14 +373,8 @@
     tile = 4 * W if H % 4 == 0 else W
     per_plane = HW // tile
 
-    def conv(weights, pick, acc, size, forward, part, planes=range(D)):
-        for z in planes:
-            rim = ([0] if z == 0 else []) + ([2] if z == D - 1 else [])
-            if forward:
-                rim = [2 - a for a in rim]
-            taps = {"all": [0, 1, 2], "rim": rim, "rest": [a for a in range(3) if a not in rim]}[part]
-            if not taps:
-                continue
+    def conv(weights, pick, acc, size, taps_of, place):
+        for z, taps in taps_of:
             low, high = min(taps), max(taps) + 1
 
             def body(q, _):
@@ -352,9 +383,9 @@
                 left = weights(pl.ds(low * 3 * size, (high - low) * 3 * size))
                 product = jnp.dot(left, right, preferred_element_type=F32)
                 for a in taps:
-                    plane = z + 2 - a if forward else z + a
+                    plane, flip = place(z, a)
                     for b in range(3):
-                        off = 2 - b if forward else b
+                        off = 2 - b if flip else b
                         spot = pl.ds(pl.multiple_of(q * tile + off * W, W), tile)
                         k = 3 * (a - low) + b
                         acc[plane, :, spot] += product[k * size : (k + 1) * size]
@@ -362,11 +393,16 @@
 
             lax.fori_loop(0, per_plane, body, 0)
 
+    def data_conv(weights, pick, planes):
+        taps_of = [(z, [a for a in range(3) if 0 <= z + a - 2 < D]) for z in planes]
+        conv(weights, pick, iacc, cb, taps_of, lambda z, a: (z + a - 1, False))
+
     def response():
         conv(
-            lambda r: wfwd[r, :], lambda lanes: vall[:, :, lanes].reshape(3 * cb * n, tile), racc, fb, True, "all"
+            lambda r: wfwd[r, :], lambda lanes: vall[:, :, lanes].reshape(3 * cb * n, tile), racc, fb,
+            [(z, [0, 1, 2]) for z in range(D)], lambda z, a: (z + 2 - a, True),
         )
-        both_ways(lambda up: rim_copy(0, up).start())
+        both_ways(lambda up: rim_copy(up).start())
 
     def kernel_swapped():
         for d in range(half):
@@ -379,111 +415,97 @@
             wl[g * W : (g + 1) * W, :] = piece.T
 
     def most_blocks():
-        conv(
-            lambda r: wst[r, :], lambda lanes: call[:, :, lanes].reshape(3 * F, tile), iacc, cb, False, "all"
-        )
-        both_ways(lambda up: rim_copy(1, up).start())
-
-    def far_rim(up):
-        plane = lc.at[far, D - 1 if up else 0]
-        k = 0 if up else 1
-        return remote(plane, lrim.at[k], ls.at[k], lr.at[k], {"sp": s + 1 if up else s - 1})
-
-    def far_use(k):
-        remote(lrim.at[k], lrim.at[k], ls.at[k], lr.at[k], {"sp": (s + 1) % S}).wait_recv()
-        x = lrim[k]
+        data_conv(lambda r: wst[r, :], lambda lanes: call[:, :, lanes].reshape(3 * F, tile), range(D + 2))
+
+    def far_shift(x, plane):
         before, after = shifts(x, W)
-        right = jnp.concatenate([after, x, before], axis=0)
-        a = 2 if k == 0 else 0
-        product = jnp.dot(wl[3 * a * cb : 3 * (a + 1) * cb, :], right, preferred_element_type=F32)
-        plane = 1 if k == 0 else D
-        for b in range(3):
-            iacc[plane, :, b * W : b * W + HW] += product[b * cb : (b + 1) * cb]
+        for c, value in enumerate((after, x, before)):
+            lcall[c * fb : (c + 1) * fb, plane * HW : (plane + 1) * HW] = value
+        data_conv(lambda r: wl[r, :], lambda lanes: lcall[:, lanes], [plane])
 
     def far_block():
         for z in range(D):
             zwait(1, last, z)
-            if z == 0:
-                @pl.when(s > 0)
+            for up in (False, True):
+                if z == (D - 1 if up else 0):
+                    for direction in range(2):
+                        @pl.when(zrecvs(direction, last) & ((s < S - 1) if up else (s > 0)))
+                        def _():
+                            brim_copy(direction, last, up).start()
+
+            far_shift(lc[far, z], z + 1)
+
+        for k in (1, 0):
+            for direction in range(2):
+                @pl.when(zrecvs(direction, last) & ((s > 0) if k == 0 else (s < S - 1)))
                 def _():
-                    far_rim(False).start()
-
-            if z == D - 1:
-                @pl.when(s < S - 1)
-                def _():
-                    far_rim(True).start()
-
-            x = lc[far, z]
-            before, after = shifts(x, W)
-            for c, value in enumerate((after, x, before)):
-                lcall[c * fb : (c + 1) * fb, z * HW : (z + 1) * HW] = value
-            conv(lambda r: wl[r, :], lambda lanes: lcall[:, lanes], iacc, cb, False, "rest", [z])
-
-        @pl.when(s < S - 1)
-        def _():
-            far_use(1)
-
-        @pl.when(s > 0)
-        def _():
-            far_use(0)
-
-        both_ways(lambda up: far_rim(up).wait_send())
-
-    def finish(which, out, acc, buf):
-        @pl.when(s > 0)
-        def _():
-            remote(buf.at[0], buf.at[0], rims.at[which, 0], rimr.at[which, 0], {"sp": (s + 1) % S}).wait_recv()
-            acc[1, :, W : W + HW] += buf[0]
-
-        @pl.when(s < S - 1)
-        def _():
-            remote(buf.at[1], buf.at[1], rims.at[which, 1], rimr.at[which, 1], {"sp": (s + 1) % S}).wait_recv()
-            acc[D, :, W : W + HW] += buf[1]
-
+                    brim_wait(direction, last, k)
+                    far_shift(lrim[k, far], 0 if k == 0 else D + 1)
+
+    def finish(out, acc):
         for z in range(D):
             out[:, z * HW : (z + 1) * HW] = acc[z + 1, :, W : W + HW].astype(BF)
 
+    def finish_response():
+        @pl.when(s > 0)
+        def _():
+            remote(rbuf.at[0], rbuf.at[0], rims.at[0], rimr.at[0], {"sp": (s + 1) % S}).wait_recv()
+            racc[1, :, W : W + HW] += rbuf[0]
+
+        @pl.when(s < S - 1)
+        def _():
+            remote(rbuf.at[1], rbuf.at[1], rims.at[1], rimr.at[1], {"sp": (s + 1) % S}).wait_recv()
+            racc[D, :, W : W + HW] += rbuf[1]
+
+        finish(resp, racc)
+
     last = n - 2
     def forwards(t):
+        for z in range(D):
+            zwait(1, t, z)
+            zstart(1, t + 1, z)
+        brims(t, lambda copy: copy.start())
+
+    forwards(0)
+    reduce_pair(1)
+    for t in range(1, last):
         @pl.when(jnp.logical_not(ends))
         def _():
-            for z in range(D):
-                zwait(1, t, z)
-                zstart(1, t + 1, z)
-
-    for t in range(last):
-        forwards(t)
-        if t == 0:
-            reduce_pair(1)
+            forwards(t)
+
+    zshift(1, 0)
     response()
     reduce_chips(0)
-    for t in range(last):
+    for t in range(1, last):
         @pl.when(ends)
         def _():
-            for z in range(D):
-                zwait(1, t, z)
+            forwards(t)
 
         zshift(1, t)
     kernel_swapped()
+    for t in range(last):
+        brims_use(t)
+    most_blocks()
     reduce_chips(1)
-    most_blocks()
     gather_forward(0)
     gather_forward(1)
-    finish(0, resp, racc, rbuf)
+    finish_response()
 
     @pl.when(ends)
     def _():
         far_block()
 
-    finish(1, igrad, iacc, ibuf)
+    finish(igrad, iacc)
     gather_end(0)
     gather_end(1)
 
     for which in range(2):
         for t in range(n - 1):
             zfinish(which, t)
-        both_ways(lambda up: rim_copy(which, up).wait_send())
     both_ways(lambda up: crim_copy(up).wait_send())
+    both_ways(lambda up: rim_copy(up).wait_send())
+    for t in range(n - 1):
+        brims(t, lambda copy: copy.wait_send())
 
     def w2_end(r, g):
         for d in range(1, half):
@@ -526,13 +548,12 @@
         out_specs=(spec,) * 3,
         scratch_shapes=[
             pltpu.VMEM((3, C, cells), BF),
-            pltpu.VMEM((3, F, cells), BF),
+            pltpu.VMEM((3, F, cells + 2 * H * W), BF),
             pltpu.VMEM((3, D + 2, fb, pads), BF),
             pltpu.VMEM((2, fb, H * W), BF),
             pltpu.VMEM((D + 2, fb, pads), F32),
             pltpu.VMEM((D + 2, cb, pads), F32),
             pltpu.VMEM((2, fb, H * W), F32),
-            pltpu.VMEM((2, cb, H * W), F32),
             pltpu.VMEM((9 * fb, 3 * C), BF),
             pltpu.VMEM((carried, n, fb, W), BF),
             pltpu.VMEM((G, F, W), BF),
@@ -540,8 +561,8 @@
             pltpu.VMEM((gpc * W, 3 * fb), BF),
             pltpu.VMEM((n, D, cb, H * W), BF),
             pltpu.VMEM((n, D, fb, H * W), BF),
-            pltpu.VMEM((2, fb, H * W), BF),
-            pltpu.VMEM((3 * fb, cells), BF),
+            pltpu.VMEM((2, n, fb, H * W), BF),
+            pltpu.VMEM((3 * fb, cells + 2 * H * W), BF),
             pltpu.VMEM((2, 2, half, R, C // 2), F32),
             pltpu.VMEM((2, half, R, C // 2), F32),
             pltpu.VMEM((2, half - 1, R, C // 2), F32),
@@ -554,8 +575,8 @@
             dma((carried, half - 1)),
             dma((2,)),
             dma((2,)),
-            dma((2, 2)),
-            dma((2, 2)),
+            dma((2,)),
+            dma((2,)),
             dma((2,)),
             dma((2,)),
             dma((2, half - 1)),
@@ -564,8 +585,8 @@
             dma((2, half - 1)),
             dma((2, half)),
             dma((2, half)),
-            dma((2,)),
-            dma((2,)),
+            dma((2, 2, n - 1)),
+            dma((2, 2, n - 1)),
             dma((carried, half)),
             dma((carried, half)),
         ],

time: 62.4 us -> 69 us (1.11)
  Pallas kernels: 57.9 us -> 64.4 us
    pallas_call x1, Pallas kernels: 57.9 us -> 64.4 us  [local(): pl.pallas_call(functools.partial(kernel, n, S, D, H, W, gpc, factor), out...]
where the time goes in v6:
time: 69 us; the launch traced here: 68.8 us
  Pallas kernels  64.4 us (93%)
  local copies, waits for them, and re-layouts  3.72 us (5%)
    pallas_call x1, Pallas kernels, local(): pl.pallas_call(functools.partial(kernel, n, S, D, H, W, gpc, factor), out...  64.4 us
    unnamed x5, local copies, waits for them, and re-layouts  2.51 us

profile of v6, /device:TPU:1, one launch (start us, length us, event | category | flops | bytes accessed | tf_op | source)
XLA Modules:
  0.0 68.8 jit_solution(17499379682956852752)
XLA Ops:
  0.6 0.0 copy-start
  0.6 1.2 %copy_bitcast_fusion = (bf16[64,2048]{1,0:T(8,128)(2,1)S(1)}, bf16[64,2048]{1,0:T(8,128)(2,1)S(1)}) fusion(bf16[8,8,16,128]{3,2,1,0:T(8,128)(2,1)} %bitcast.26, bf16[8,8,16,128]{3,2,1,0:T(8,128)(2,1)} %bitcast.27), kind=kLoop, calls=%fused_computation | loop fusion | bytes 1048576 | tf_op jit(solution)/shard_map/reshape | solution.py:596
  1.9 0.1 copy-done
  2.0 64.4 %shard_map.58 = (bf16[64,2048]{1,0:T(8,128)(2,1)S(1)}, bf16[64,2048]{1,0:T(8,128)(2,1)S(1)}, bf16[1728,256]{1,0:T(8,128)(2,1)S(1)}) custom-call(bf16[64,2048]{1,0:T(8,128)(2,1)S(1)} %get-tuple-element.10.vol, bf16[64,2048]{1,0:T(8,128)(2,1)S(1)} %get-tuple-element.9.cot, bf16[27,64,256]{2,1,0:T(8,128)(2,1)S(1)} %bitcast.21), custom_call_target="tpu_custom_call" | custom-call | tf_op jit(solution)/shard_map/pallas_call | solution.py:540
  66.4 0.7 %copy.8 = bf16[8,8,16,128]{3,2,1,0:T(8,128)(2,1)} copy(bf16[8,8,16,128]{3,1,2,0:T(8,128)(2,1)S(1)} %bitcast.23) | data formatting | bytes 524288
  67.2 0.7 %copy.9 = bf16[8,8,16,128]{3,2,1,0:T(8,128)(2,1)} copy(bf16[8,8,16,128]{3,1,2,0:T(8,128)(2,1)S(1)} %bitcast.22) | data formatting | bytes 524288
  67.9 0.9 %copy.13 = bf16[64,3,3,3,256]{4,0,3,2,1:T(8,128)(2,1)} copy(bf16[64,3,3,3,256]{4,0,3,2,1:T(8,128)(2,1)S(1)} %bitcast.20) | data formatting | bytes 1769472
Async XLA Ops:
  0.6 1.3 %copy-start = (bf16[64,3,3,3,256]{4,0,3,2,1:T(8,128)(2,1)S(1)}, bf16[64,3,3,3,256]{4,0,3,2,1:T(8,128)(2,1)}, u32[]{:S(2)}) copy-start(bf16[64,3,3,3,256]{4,0,3,2,1:T(8,128)(2,1)} %param.4) | copy-start | bytes 2654212

commit v7 on v6

--- a/solution.py
+++ b/solution.py
@@ -483,11 +483,11 @@
 
         zshift(1, t)
     kernel_swapped()
+    reduce_chips(1)
+    gather_forward(0)
     for t in range(last):
         brims_use(t)
     most_blocks()
-    reduce_chips(1)
-    gather_forward(0)
     gather_forward(1)
     finish_response()
 

time: 69 us -> 65.5 us (0.949)
  Pallas kernels: 64.4 us -> 60.8 us
    pallas_call x1, Pallas kernels: 64.4 us -> 60.8 us  [local(): pl.pallas_call(functools.partial(kernel, n, S, D, H, W, gpc, factor), out...]
where the time goes in v7:
time: 65.5 us; the launch traced here: 65.2 us
  Pallas kernels  60.8 us (93%)
  local copies, waits for them, and re-layouts  3.72 us (6%)
    pallas_call x1, Pallas kernels, local(): pl.pallas_call(functools.partial(kernel, n, S, D, H, W, gpc, factor), out...  60.8 us
    unnamed x5, local copies, waits for them, and re-layouts  2.51 us

profile of v7, /device:TPU:1, one launch (start us, length us, event | category | flops | bytes accessed | tf_op | source)
XLA Modules:
  0.0 65.2 jit_solution(16805667495004033391)
XLA Ops:
  0.6 0.0 copy-start
  0.6 1.2 %copy_bitcast_fusion = (bf16[64,2048]{1,0:T(8,128)(2,1)S(1)}, bf16[64,2048]{1,0:T(8,128)(2,1)S(1)}) fusion(bf16[8,8,16,128]{3,2,1,0:T(8,128)(2,1)} %bitcast.26, bf16[8,8,16,128]{3,2,1,0:T(8,128)(2,1)} %bitcast.27), kind=kLoop, calls=%fused_computation | loop fusion | bytes 1048576 | tf_op jit(solution)/shard_map/reshape | solution.py:596
  1.9 0.1 copy-done
  2.0 60.8 %shard_map.58 = (bf16[64,2048]{1,0:T(8,128)(2,1)S(1)}, bf16[64,2048]{1,0:T(8,128)(2,1)S(1)}, bf16[1728,256]{1,0:T(8,128)(2,1)S(1)}) custom-call(bf16[64,2048]{1,0:T(8,128)(2,1)S(1)} %get-tuple-element.10.vol, bf16[64,2048]{1,0:T(8,128)(2,1)S(1)} %get-tuple-element.9.cot, bf16[27,64,256]{2,1,0:T(8,128)(2,1)S(1)} %bitcast.21), custom_call_target="tpu_custom_call" | custom-call | tf_op jit(solution)/shard_map/pallas_call | solution.py:540
  62.8 0.7 %copy.8 = bf16[8,8,16,128]{3,2,1,0:T(8,128)(2,1)} copy(bf16[8,8,16,128]{3,1,2,0:T(8,128)(2,1)S(1)} %bitcast.23) | data formatting | bytes 524288
  63.5 0.7 %copy.9 = bf16[8,8,16,128]{3,2,1,0:T(8,128)(2,1)} copy(bf16[8,8,16,128]{3,1,2,0:T(8,128)(2,1)S(1)} %bitcast.22) | data formatting | bytes 524288
  64.3 0.9 %copy.13 = bf16[64,3,3,3,256]{4,0,3,2,1:T(8,128)(2,1)} copy(bf16[64,3,3,3,256]{4,0,3,2,1:T(8,128)(2,1)S(1)} %bitcast.20) | data formatting | bytes 1769472
Async XLA Ops:
  0.6 1.3 %copy-start = (bf16[64,3,3,3,256]{4,0,3,2,1:T(8,128)(2,1)S(1)}, bf16[64,3,3,3,256]{4,0,3,2,1:T(8,128)(2,1)}, u32[]{:S(2)}) copy-start(bf16[64,3,3,3,256]{4,0,3,2,1:T(8,128)(2,1)} %param.4) | copy-start | bytes 2654212
